TPU v7x, 32 devices: a whole 2x2x4 slice. The times are simulated.
32 devices in a mesh: gx: 8 (over z, core), yz: 4 (over y, x).
Axes of the slice: x: 2, y: 2, z: 4, core: 2. Of those that a mesh axis runs over, the one named last changes fastest.
Arguments:
- state: float32 [5, 128, 64, 256], P(None, 'gx', 'yz'), may hold values from -3 to 9, as said below
- register: float32 [5, 128, 64, 256], P(None, 'gx', 'yz'), may hold values from -4 to 4
Outputs:
- register_out: float32 [5, 128, 64, 256], P(None, 'gx', 'yz')
- filtered: float32 [5, 128, 64, 256], P(None, 'gx', 'yz')
Inputs may be any that keep to these rules, and one draw needn't show every extreme that they name: state holds the density, the three momenta and the total energy of an ideal gas with ratio of specific heats 1.4; in every cell the density lies between 0.4 and 2.2 and the pressure between 0.4 and 2.1.
All inputs are finite; a program needn't handle non-finite values.
Results may differ from a plain program's by a relative error of at most 0.0003.
Values sent between devices are 32-bit elements; how exact they have to be, the bound alone decides.
A program may use at most 128 MiB of HBM per device.

v0:
```python
import jax
import jax.numpy as jnp
from jax import lax
from jax.sharding import PartitionSpec as P

gamma_gas = 1.4
central_weights = (4.0 / 5.0, -1.0 / 5.0, 4.0 / 105.0, -1.0 / 280.0)
filter_alpha = 0.49
register_decay = -5.0 / 9.0
register_gain = 15.0 / 16.0
time_step = 0.2


def with_halo(cells, sides, width):
    for axis, dim in sides:
        count = lax.axis_size(axis)
        head = lax.slice_in_dim(cells, 0, width, axis=dim)
        tail = lax.slice_in_dim(cells, cells.shape[dim] - width, cells.shape[dim], axis=dim)
        cells = jnp.concatenate(
            [
                lax.ppermute(tail, axis, [(i, (i + 1) % count) for i in range(count)]),
                cells,
                lax.ppermute(head, axis, [((i + 1) % count, i) for i in range(count)]),
            ],
            axis=dim,
        )
    return cells


def primitives(fields):
    density = fields[0]
    speed_x = fields[1] / density
    speed_y = fields[2] / density
    speed_z = fields[3] / density
    kinetic = 0.5 * density * (speed_x * speed_x + speed_y * speed_y + speed_z * speed_z)
    pressure = (gamma_gas - 1.0) * (fields[4] - kinetic)
    enthalpy = (fields[4] + pressure) / density
    return (density, speed_x, speed_y, speed_z, pressure, enthalpy)


def pair_flux(left, right, direction):
    means = [0.5 * (one + other) for one, other in zip(left, right)]
    density, speed_x, speed_y, speed_z, pressure, enthalpy = means
    normal = (speed_x, speed_y, speed_z)[direction]
    mass = density * normal
    moment = [mass * speed_x, mass * speed_y, mass * speed_z]
    moment[direction] = moment[direction] + pressure
    return [mass] + moment + [mass * enthalpy]


def residual_of(padded):
    width_x = padded.shape[1] - 8
    width_y = padded.shape[2] - 8
    along_x = primitives(padded[:, :, 4:-4])
    along_y = primitives(padded[:, 4:-4, :])
    center = tuple((column[4:-4] for column in along_x))
    total = [jnp.zeros_like(center[0]) for field in range(5)]
    for offset in range(1, 5):
        weight = central_weights[offset - 1]
        left = tuple((column[:-offset] for column in along_x))
        right = tuple((column[offset:] for column in along_x))
        flux = pair_flux(left, right, 0)
        total = [
            part
            - 2.0 * weight * (value[4 : 4 + width_x] - value[4 - offset : 4 - offset + width_x])
            for part, value in zip(total, flux)
        ]
    for offset in range(1, 5):
        weight = central_weights[offset - 1]
        left = tuple((column[:, :-offset] for column in along_y))
        right = tuple((column[:, offset:] for column in along_y))
        flux = pair_flux(left, right, 1)
        total = [
            part
            - 2.0
            * weight
            * (value[:, 4 : 4 + width_y] - value[:, 4 - offset : 4 - offset + width_y])
            for part, value in zip(total, flux)
        ]
    for offset in range(1, 5):
        weight = central_weights[offset - 1]
        ahead = tuple((jnp.roll(column, -offset, axis=2) for column in center))
        flux = pair_flux(center, ahead, 2)
        total = [
            part - 2.0 * weight * (value - jnp.roll(value, offset, axis=2))
            for part, value in zip(total, flux)
        ]
    return jnp.stack(total)


def filter_rhs(extended):
    coeffs = (
        (11.0 + 10.0 * filter_alpha) / 16.0,
        (15.0 + 34.0 * filter_alpha) / 32.0,
        (-3.0 + 6.0 * filter_alpha) / 16.0,
        (1.0 - 2.0 * filter_alpha) / 32.0,
    )
    width_x = extended.shape[1] - 6
    rhs = coeffs[0] * extended[:, 3 : 3 + width_x]
    for shift in range(1, 4):
        rhs = rhs + coeffs[shift] / 2.0 * (
            extended[:, 3 + shift : 3 + shift + width_x]
            + extended[:, 3 - shift : 3 - shift + width_x]
        )
    return rhs


def line_solve(rhs, share, own):
    highest = lax.Precision.HIGHEST
    inner = rhs.shape[1] - 1
    places = jnp.arange(inner)
    lower = jnp.where(places == 0, 0.0, filter_alpha).astype(jnp.float32)
    upper = jnp.where(places == inner - 1, 0.0, filter_alpha).astype(jnp.float32)
    middle = jnp.ones((inner,), jnp.float32)
    inverse = lax.linalg.tridiagonal_solve(lower, middle, upper, jnp.eye(inner, dtype=jnp.float32))
    interior = jnp.einsum("ij,fjyz->fiyz", inverse, rhs[:, :inner], precision=highest)
    first = interior[:, 0]
    partial_rhs = rhs[:, inner] - filter_alpha * interior[:, inner - 1]
    pairs = jnp.stack([first, partial_rhs])[None]
    gathered = share(pairs)
    count = gathered.shape[0]
    coupled = gathered[:, 1] - filter_alpha * jnp.roll(gathered[:, 0], -1, axis=0)
    diagonal = 1.0 - 2.0 * filter_alpha * filter_alpha * inverse[0, 0]
    across = -filter_alpha * filter_alpha * inverse[inner - 1, 0]
    cycle = jnp.arange(count)
    following = (cycle[None, :] == (cycle[:, None] + 1) % count).astype(jnp.float32)
    system = diagonal * jnp.eye(count, dtype=jnp.float32) + across * (following + following.T)
    factor = jnp.linalg.cholesky(system)
    system_inverse = jax.scipy.linalg.cho_solve((factor, True), jnp.eye(count, dtype=jnp.float32))
    before_row = lax.dynamic_index_in_dim(
        system_inverse, (own + count - 1) % count, 0, keepdims=False
    )
    own_row = lax.dynamic_index_in_dim(system_inverse, own, 0, keepdims=False)
    rows = jnp.stack([before_row, own_row])
    separators = jnp.einsum("kp,pfyz->kfyz", rows, coupled, precision=highest)
    before_sep = separators[0]
    own_sep = separators[1]
    solved = interior - filter_alpha * (
        before_sep[:, None] * inverse[:, 0][None, :, None, None]
        + own_sep[:, None] * inverse[:, inner - 1][None, :, None, None]
    )
    return jnp.concatenate([solved, own_sep[:, None]], axis=1)


def body(state, register):
    padded = with_halo(state, (("gx", 1), ("yz", 2)), 4)
    residual = residual_of(padded)
    register_out = register_decay * register + time_step * residual
    section = state + register_gain * register_out
    extended = with_halo(section, (("gx", 1),), 3)
    rhs = filter_rhs(extended)

    def share(pairs):
        return lax.all_gather(pairs, "gx", axis=0, tiled=True)

    filtered = line_solve(rhs, share, lax.axis_index("gx"))
    return (register_out, filtered)


def solution(mesh):
    in_specs = (P(None, "gx", "yz", None), P(None, "gx", "yz", None))
    out_specs = (P(None, "gx", "yz", None), P(None, "gx", "yz", None))
    return jax.shard_map(body, mesh=mesh, in_specs=in_specs, out_specs=out_specs, check_vma=False)
```

profile of v0, /device:TPU:0, one launch (start us, length us, event | category | flops | bytes accessed | tf_op | source)
XLA Modules:
  0.0 123.3 jit_solution(6580971372052143502)
XLA Ops:
  7.2 2.1 %copy.33 = f32[5,16,16,256]{3,1,2,0:T(8,128)S(1)} copy(f32[5,16,16,256]{3,2,1,0:T(8,128)} %param.2) | data formatting | bytes 2621440 | tf_op args[0]
  9.3 0.9 fusion.357
  10.2 4.5 %collective-permute-start.1 = (f32[5,4,16,256]{3,1,2,0:T(4,128)}, f32[5,4,16,256]{3,1,2,0:T(4,128)S(1)}, u32[]{:S(2)}, u32[]{:S(2)}) collective-permute-start(f32[5,4,16,256]{3,1,2,0:T(4,128)} %get-tuple-element.86), channel_id=1, source_target_pairs={{4,0},{8,4},{12,8},{16,12},{20,16},{24,20},{28,24},{0,28},{5,1},{9... | collective-permute-start | bytes 983048 | tf_op jit(solution)/shard_map/ppermute | solution.py:23
  15.6 0.7 fusion.360
  16.3 0.7 fusion.359
  37.7 2.5 %collective-permute-start.3 = (f32[5,24,4,256]{3,1,2,0:T(8,128)S(1)}, f32[5,24,4,256]{3,1,2,0:T(8,128)S(1)}, u32[]{:S(2)}, u32[]{:S(2)}) collective-permute-start(f32[5,24,4,256]{3,1,2,0:T(8,128)S(1)} %get-tuple-element.80), channel_id=1, source_target_pairs={{1,0},{2,1},{3,2},{0,3},{5,4},{6,5},{7,6},{4,7},{9,8},{10,9},{11,1... | collective-permute-start | bytes 1474568 | tf_op jit(solution)/shard_map/ppermute | solution.py:23
  46.5 5.5 %collective-permute-done.3 = f32[5,24,4,256]{3,1,2,0:T(8,128)S(1)} collective-permute-done((f32[5,24,4,256]{3,1,2,0:T(8,128)S(1)}, f32[5,24,4,256]{3,1,2,0:T(8,128)S(1)}, u32[]{:S(2)}, u32[]{:S(2)}) %collective-permute-start.3) | collective-permute-done | bytes 491552 | tf_op jit(solution)/shard_map/ppermute | solution.py:23
  51.9 9.1 %collective-permute-done.2 = f32[5,24,4,256]{3,1,2,0:T(8,128)S(1)} collective-permute-done((f32[5,24,4,256]{3,1,2,0:T(8,128)S(1)}, f32[5,24,4,256]{3,1,2,0:T(8,128)S(1)}, u32[]{:S(2)}, u32[]{:S(2)}) %collective-permute-start.2) | collective-permute-done | bytes 491552 | tf_op jit(solution)/shard_map/ppermute | solution.py:21
  65.9 0.7 copy-done.1
  67.0 2.0 %multiply_add_fusion = (f32[5,16,16,256]{3,1,2,0:T(8,128)S(1)}, f32[5,16,16,256]{3,1,2,0:T(8,128)S(1)}) fusion(f32[5,16,16,256]{3,2,1,0:T(8,128)S(1)} %copy-done.1, f32[5,16,16,256]{3,1,2,0:T(8,128)S(1)} %fusion.128, f32[5,16,16,256]{3,2,1,0:T(8,128)S(1)} %copy-done.3), kind=kLoop, calls=%fused_computation.30 | loop fusion | flops 1638400 | bytes 6553600 | tf_op jit(solution)/shard_map/add | solution.py:149
  69.0 0.8 fusion.356
  69.9 3.5 %collective-permute-start.4 = (f32[5,3,16,256]{3,1,2,0:T(4,128)S(1)}, f32[5,3,16,256]{3,1,2,0:T(4,128)}, u32[]{:S(2)}, u32[]{:S(2)}) collective-permute-start(f32[5,3,16,256]{3,1,2,0:T(4,128)S(1)} %get-tuple-element.83), channel_id=1, source_target_pairs={{4,0},{8,4},{12,8},{16,12},{20,16},{24,20},{28,24},{0,28},{5,1},{9... | collective-permute-start | bytes 737288 | tf_op jit(solution)/shard_map/ppermute | solution.py:23
  73.4 8.2 %fusion.308 = (f32[1,15]{1,0:T(1,128)S(1)}, f32[1,15]{1,0:T(1,128)S(1)}, f32[1,15]{1,0:T(1,128)S(1)}, f32[1,15]{1,0:T(1,128)S(1)}, f32[1,15]{1,0:T(1,128)S(1)}, ...) fusion(f32[15,15]{1,0:T(8,128)S(1)} %fusion.298, ...), kind=kLoop, calls=%fused_computation.503 | loop fusion | flops 585 | bytes 1724 | tf_op jit(solution)/shard_map/eval_jaxpr/div | solution.py:115
  82.9 1.3 %multiply_subtract_fusion.1 = (f32[1,15]{1,0:T(1,128)S(1)}, f32[1,15]{1,0:T(1,128)S(1)}, f32[1,15]{1,0:T(1,128)S(1)}, f32[1,15]{1,0:T(1,128)S(1)}, f32[1,15]{1,0...) fusion(f32[15,15]{1,0:T(8,128)S(1)} %fusion.298, ...), kind=kLoop, calls=%fused_computation.528 | loop fusion | flops 465 | bytes 1864 | tf_op jit(solution)/shard_map/eval_jaxpr/sub | solution.py:115
  84.3 2.6 %fusion.4 = f32[5,16,16,256]{3,1,2,0:T(8,128)S(1)} fusion(f32[5,16,16,256]{3,1,2,0:T(8,128)S(1)} %get-tuple-element.38, f32[5,3,16,256]{3,1,2,0:T(4,128)S(1)} %collective-permute-done.5, f32[5,3,16,256]{3,1,2,0:T(4,128)} %collective-permute-done.4), kind=kLoop, calls=%fused_computation.14 | loop fusion | flops 5242880 | bytes 3112960 | tf_op jit(solution)/shard_map/add | solution.py:101
  86.9 1.2 %convolution_bitcast_fusion = f32[5,15,16,256]{3,1,2,0:T(8,128)S(1)} fusion(f32[5,16,16,256]{3,1,2,0:T(8,128)S(1)} %fusion.4, f32[15,15]{1,0:T(8,128)S(1)} %concatenate.223), kind=kOutput, calls=%fused_computation.9 | convolution fusion | flops 55296000 | bytes 2540420 | tf_op jit(solution)/shard_map/ij,fjyz->fiyz/dot_general | solution.py:116
  88.5 0.7 copy.41
  89.4 0.7 cholesky.17
  92.6 1.8 %copy.45 = f32[5,16,16,256]{3,2,1,0:T(8,128)} copy(f32[5,16,16,256]{3,1,2,0:T(8,128)S(1)} %get-tuple-element.39) | data formatting | bytes 2621440
  94.4 15.9 %all-gather.3.cloned.1.call-done = f32[16,5,16,256]{3,2,1,0:T(8,128)} async-done(((f32[2,5,16,256]{3,2,1,0:T(8,128)}), f32[16,5,16,256]{3,2,1,0:T(8,128)}) %all-gather.3.cloned.1.call-update) | async-done | bytes 1310736 | tf_op jit(solution)/shard_map/all_gather | solution.py:154
  110.2 1.0 slice.2319
  111.2 1.1 slice.2318
  112.8 1.1 fusion.16
  114.7 1.8 %copy.46 = f32[5,16,16,256]{3,2,1,0:T(8,128)} copy(f32[5,16,16,256]{3,1,2,0:T(8,128)S(1)} %pad_maximum_fusion.3) | data formatting | bytes 2621440
  (143 shorter events, 20.1 us)
Async XLA Ops:
  7.2 103.1 %all-gather.3.cloned.1.call-start = ((), (), s32[]{:S(2)}) async-start(), calls=%async_computation | async-start | bytes 1474560 | tf_op jit(solution)/shard_map/all_gather | solution.py:154
  10.2 23.2 %collective-permute-start.1 = (f32[5,4,16,256]{3,1,2,0:T(4,128)}, f32[5,4,16,256]{3,1,2,0:T(4,128)S(1)}, u32[]{:S(2)}, u32[]{:S(2)}) collective-permute-start(f32[5,4,16,256]{3,1,2,0:T(4,128)} %get-tuple-element.86), channel_id=1, source_target_pairs={{4,0},{8,4},{12,8},{16,12},{20,16},{24,20},{28,24},{0,28},{5,1},{9... | collective-permute-start | bytes 983048 | tf_op jit(solution)/shard_map/ppermute | solution.py:23
  14.7 18.7 %collective-permute-start = (f32[5,4,16,256]{3,1,2,0:T(4,128)}, f32[5,4,16,256]{3,1,2,0:T(4,128)S(1)}, u32[]{:S(2)}, u32[]{:S(2)}) collective-permute-start(f32[5,4,16,256]{3,1,2,0:T(4,128)} %get-tuple-element.85), channel_id=1, source_target_pairs={{0,4},{4,8},{8,12},{12,16},{16,20},{20,24},{24,28},{28,0},{1,5},{5... | collective-permute-start | bytes 983048 | tf_op jit(solution)/shard_map/ppermute | solution.py:21
  14.7 0.7 copy-start
  37.2 3.0 %slice-start = ((f32[16,16,256]{2,0,1:T(8,128)}), f32[16,16,3]{2,0,1:T(8,128)S(1)}, s32[]{:S(2)}) async-start(f32[16,16,256]{2,0,1:T(8,128)} %copy-done), calls=%async_computation.1 | async-start | bytes 262144 | tf_op jit(solution)/shard_map/jit(_roll_static)/slice | solution.py:82
  37.2 3.0 %slice-start.1 = ((f32[16,16,256]{2,0,1:T(8,128)}), f32[16,16,1]{2,0,1:T(8,128)S(1)}, s32[]{:S(2)}) async-start(f32[16,16,256]{2,0,1:T(8,128)} %copy-done), calls=%async_computation.2 | async-start | bytes 262144 | tf_op jit(solution)/shard_map/jit(_roll_static)/slice | solution.py:82
  37.7 14.2 %collective-permute-start.3 = (f32[5,24,4,256]{3,1,2,0:T(8,128)S(1)}, f32[5,24,4,256]{3,1,2,0:T(8,128)S(1)}, u32[]{:S(2)}, u32[]{:S(2)}) collective-permute-start(f32[5,24,4,256]{3,1,2,0:T(8,128)S(1)} %get-tuple-element.80), channel_id=1, source_target_pairs={{1,0},{2,1},{3,2},{0,3},{5,4},{6,5},{7,6},{4,7},{9,8},{10,9},{11,1... | collective-permute-start | bytes 1474568 | tf_op jit(solution)/shard_map/ppermute | solution.py:23
  40.2 0.9 slice-start.2
  40.2 1.0 slice-start.3
  40.2 20.8 %collective-permute-start.2 = (f32[5,24,4,256]{3,1,2,0:T(8,128)S(1)}, f32[5,24,4,256]{3,1,2,0:T(8,128)S(1)}, u32[]{:S(2)}, u32[]{:S(2)}) collective-permute-start(f32[5,24,4,256]{3,1,2,0:T(8,128)S(1)} %get-tuple-element.79), channel_id=1, source_target_pairs={{0,1},{1,2},{2,3},{3,0},{4,5},{5,6},{6,7},{7,4},{8,9},{9,10},{10,1... | collective-permute-start | bytes 1474568 | tf_op jit(solution)/shard_map/ppermute | solution.py:21
  65.3 1.3 %copy-start.1 = (f32[5,16,16,256]{3,2,1,0:T(8,128)S(1)}, f32[5,16,16,256]{3,2,1,0:T(8,128)}, u32[]{:S(2)}) copy-start(f32[5,16,16,256]{3,2,1,0:T(8,128)} %param.2) | copy-start | bytes 3932164
  65.3 1.7 %copy-start.3 = (f32[5,16,16,256]{3,2,1,0:T(8,128)S(1)}, f32[5,16,16,256]{3,2,1,0:T(8,128)}, u32[]{:S(2)}) copy-start(f32[5,16,16,256]{3,2,1,0:T(8,128)} %param.3) | copy-start | bytes 3932164
  69.9 14.4 %collective-permute-start.5 = (f32[5,3,16,256]{3,1,2,0:T(4,128)}, f32[5,3,16,256]{3,1,2,0:T(4,128)S(1)}, u32[]{:S(2)}, u32[]{:S(2)}) collective-permute-start(f32[5,3,16,256]{3,1,2,0:T(4,128)} %get-tuple-element.84), channel_id=1, source_target_pairs={{0,4},{4,8},{8,12},{12,16},{16,20},{20,24},{24,28},{28,0},{1,5},{5... | collective-permute-start | bytes 737288 | tf_op jit(solution)/shard_map/ppermute | solution.py:21
  69.9 14.4 %collective-permute-start.4 = (f32[5,3,16,256]{3,1,2,0:T(4,128)S(1)}, f32[5,3,16,256]{3,1,2,0:T(4,128)}, u32[]{:S(2)}, u32[]{:S(2)}) collective-permute-start(f32[5,3,16,256]{3,1,2,0:T(4,128)S(1)} %get-tuple-element.83), channel_id=1, source_target_pairs={{4,0},{8,4},{12,8},{16,12},{20,16},{24,20},{28,24},{0,28},{5,1},{9... | collective-permute-start | bytes 737288 | tf_op jit(solution)/shard_map/ppermute | solution.py:23
  110.2 2.1 %copy-start.2 = (f32[16,5,16,256]{3,2,1,0:T(8,128)S(1)}, f32[16,5,16,256]{3,2,1,0:T(8,128)}, u32[]{:S(2)}) copy-start(f32[16,5,16,256]{3,2,1,0:T(8,128)} %all-gather.3.cloned.1.call-done) | copy-start | bytes 3932164
Sparse Core Ops, SparseCore 0:
  89.3 20.8 all-gather.2
where the time goes:
time: 124 us; the launch traced here: 123 us
  between operations  32.8 us (26%)
  waiting for transfers between devices  30.4 us (25%)
  other arithmetic  27 us (22%)
  local copies, waits for them, and re-layouts  19.8 us (16%)
  starting transfers between devices  10.6 us (9%)
  matrix products  2.68 us (2%)
    all_gather x1, waiting for transfers between devices, share(): return lax.all_gather(pairs, 'gx', axis=0, tiled=True)  15.9 us
    ppermute x3, starting transfers between devices, with_halo(): lax.ppermute(head, axis, [((i + 1) % count, i) for i in range(count)])  10.5 us
    ppermute x3, waiting for transfers between devices, with_halo(): lax.ppermute(tail, axis, [(i, (i + 1) % count) for i in range(count)])  9.11 us
    div x1, other arithmetic, line_solve(): lax.linalg.tridiagonal_solve(lower, middle, upper, jnp.eye(inner, dtype=j...  8.17 us
    unnamed x14, local copies, waits for them, and re-layouts  7.54 us
    ppermute x3, waiting for transfers between devices, with_halo(): lax.ppermute(head, axis, [((i + 1) % count, i) for i in range(count)])  5.46 us
    slice x52, local copies, waits for them, and re-layouts, residual_of(): ahead = tuple((jnp.roll(column, -offset, axis=2) for column in center))  3.9 us
    mul x10, other arithmetic, pair_flux(): moment = [mass * speed_x, mass * speed_y, mass * speed_z]  2.69 us
  transfers between devices with their start and end apart: 7, of which 3 were waited for; matrix products, arithmetic and copies ran while one was open for 18% of the time, Pallas kernels for 0%

commit v1 on v0

v1 whole, which is shorter than its diff:
```python
import functools

import jax
import jax.numpy as jnp
from jax import lax
from jax.experimental import pallas as pl
from jax.experimental.pallas import tpu as pltpu
from jax.sharding import PartitionSpec as P

gamma_gas = 1.4
central_weights = (4.0 / 5.0, -1.0 / 5.0, 4.0 / 105.0, -1.0 / 280.0)
filter_alpha = 0.49
register_decay = -5.0 / 9.0
register_gain = 15.0 / 16.0
time_step = 0.2
MESH = pl.DeviceIdType.MESH
LANES = 128
ROWS = 8


def filter_constants():
    alpha = filter_alpha
    a0 = (11.0 + 10.0 * alpha) / 16.0
    a1 = (15.0 + 34.0 * alpha) / 32.0
    a2 = (-3.0 + 6.0 * alpha) / 16.0
    a3 = (1.0 - 2.0 * alpha) / 32.0
    q2 = 4.0 * a3 / (2.0 * alpha)
    q1 = (2.0 * a2 - q2) / (2.0 * alpha)
    q0 = (a1 - 3.0 * a3 - q1) / (2.0 * alpha)
    rest = a0 - a2 - q0
    mu = (-1.0 + (1.0 - 4.0 * alpha * alpha) ** 0.5) / (2.0 * alpha)
    kappa = (1.0 + mu * mu) / (1.0 - mu * mu)
    return (q0 + 0.5 * q2, 0.5 * q1, 0.25 * q2), kappa * rest, mu


def primitives(fields):
    density = fields[0]
    inverse = 1.0 / density
    speeds = [fields[i] * inverse for i in (1, 2, 3)]
    kinetic = 0.5 * (
        fields[1] * speeds[0] + fields[2] * speeds[1] + fields[3] * speeds[2]
    )
    pressure = (gamma_gas - 1.0) * (fields[4] - kinetic)
    enthalpy = (fields[4] + pressure) * (0.5 * inverse)
    return [density] + [0.5 * speed for speed in speeds] + [pressure, enthalpy]


def pair_flux(left, right, direction, weight):
    density, speed_x, speed_y, speed_z, pressure, enthalpy = [
        one + other for one, other in zip(left, right)
    ]
    normal = (speed_x, speed_y, speed_z)[direction]
    mass = (weight * density) * normal
    moment = [mass * speed_x, mass * speed_y, mass * speed_z]
    moment[direction] = moment[direction] + weight * pressure
    return [mass] + moment + [mass * enthalpy]


def kernel(
    n_gx,
    n_yz,
    state,
    register,
    out_register,
    out_filtered,
    reg,
    prims,
    acc,
    xrecv,
    ysend,
    yrecv,
    sec,
    regout,
    filt,
    srecv,
    ab,
    pab,
    chip,
    chips,
    inc,
    pinc,
    xs,
    xr,
    ys,
    yr,
    ss,
    sr,
    abs_,
    abr,
    cs,
    cr,
    ins,
    inr,
    local,
):
    nf, nx, ny, nz = state.shape
    n_ch = nz // LANES
    tiles = ny // ROWS
    zs = n_gx // 2
    me = lax.axis_index("gx")
    mine = lax.axis_index("yz")
    core = lax.rem(me, 2)
    chip_at = lax.div(me, 2)
    nxt = lax.rem(me + 1, n_gx)
    prv = lax.rem(me + n_gx - 1, n_gx)
    partner = me + 1 - 2 * core
    ynxt = lax.rem(mine + 1, n_yz)
    yprv = lax.rem(mine + n_yz - 1, n_yz)

    def chip_peer(d):
        return 2 * lax.rem(chip_at + (1 - 2 * core) * d + zs, zs) + core

    barrier = pltpu.get_barrier_semaphore()
    peers = [(prv, mine), (nxt, mine), (me, yprv), (me, ynxt)]
    peers += [(chip_peer(d), mine) for d in range(1, zs)]
    for peer in peers:
        pl.semaphore_signal(barrier, inc=1, device_id=peer, device_id_type=MESH)

    get_register = pltpu.make_async_copy(register, reg, local.at[0])
    get_register.start()

    @pl.loop(0, nx)
    def _(x):
        for ch in range(n_ch):
            cols = pl.ds(ch * LANES, LANES)
            for f in range(nf):
                ysend[ch, 0, f, x] = state[f, x, pl.ds(0, ROWS), cols][:4]
                ysend[ch, 1, f, x] = state[f, x, pl.ds(ny - ROWS, ROWS), cols][4:]

    pl.semaphore_wait(barrier, len(peers))

    def remote(src, dst, send, recv, peer):
        return pltpu.make_async_remote_copy(
            src_ref=src,
            dst_ref=dst,
            send_sem=send,
            recv_sem=recv,
            device_id=peer,
            device_id_type=MESH,
        )

    def y_copies(ch):
        return [
            remote(
                ysend.at[ch, side],
                yrecv.at[ch, side],
                ys.at[ch, side],
                yr.at[ch, side],
                (me, (yprv, ynxt)[side]),
            )
            for side in range(2)
        ]

    ycopies = [y_copies(ch) for ch in range(n_ch)]
    xcopies = [
        remote(state.at[:, pl.ds(0, 4)], xrecv.at[0], xs.at[0], xr.at[0], (prv, mine)),
        remote(state.at[:, pl.ds(nx - 4, 4)], xrecv.at[1], xs.at[1], xr.at[1], (nxt, mine)),
    ]
    for copy in ycopies[0] + xcopies:
        copy.start()
    for ch in range(1, n_ch):
        for copy in ycopies[ch]:
            copy.start()

    weights = [-time_step * w for w in central_weights]

    @pl.loop(0, nx * tiles)
    def _(i):
        x = i // tiles
        rows = pl.ds(pl.multiple_of((i % tiles) * ROWS, ROWS), ROWS)
        own = primitives([state[f, x, rows, :] for f in range(nf)])
        for f in range(6):
            prims[f, x + 4, rows, :] = own[f]
        total = [jnp.zeros((ROWS, nz), jnp.float32) for _ in range(nf)]
        for l in range(1, 5):
            ahead = [pltpu.roll(q, nz - l, axis=1) for q in own]
            flux = pair_flux(own, ahead, 2, weights[l - 1])
            total = [t + (v - pltpu.roll(v, l, axis=1)) for t, v in zip(total, flux)]
        for f in range(nf):
            acc[f, x, rows, :] = total[f]

    for copy in xcopies:
        copy.wait_recv()

    @pl.loop(0, 4 * tiles)
    def _(i):
        x = i // tiles
        rows = pl.ds(pl.multiple_of((i % tiles) * ROWS, ROWS), ROWS)
        for side in range(2):
            got = primitives([xrecv[side, f, x, rows, :] for f in range(nf)])
            for f in range(6):
                prims[f, x + (nx + 4, 0)[side], rows, :] = got[f]

    @pl.loop(0, nx * tiles)
    def _(i):
        x = i // tiles
        rows = pl.ds(pl.multiple_of((i % tiles) * ROWS, ROWS), ROWS)
        for ch in range(n_ch):
            cols = pl.ds(ch * LANES, LANES)
            own = [prims[f, x + 4, rows, cols] for f in range(6)]
            total = [acc[f, x, rows, cols] for f in range(nf)]
            for l in range(1, 5):
                ahead = [prims[f, x + 4 + l, rows, cols] for f in range(6)]
                behind = [prims[f, x + 4 - l, rows, cols] for f in range(6)]
                up = pair_flux(own, ahead, 0, weights[l - 1])
                down = pair_flux(behind, own, 0, weights[l - 1])
                total = [t + (u - d) for t, u, d in zip(total, up, down)]
            for f in range(nf):
                acc[f, x, rows, cols] = total[f]

    get_register.wait()

    stencil, remainder, mu = filter_constants()
    rho = mu**nx
    span = ny + ROWS

    def section_of(ch):
        cols = pl.ds(ch * LANES, LANES)
        for copy in ycopies[ch]:
            copy.wait_recv()

        @pl.loop(0, nx)
        def _(x):
            halo = primitives(
                [
                    jnp.concatenate([yrecv[ch, 0, f, x], yrecv[ch, 1, f, x]], axis=0)
                    for f in range(nf)
                ]
            )
            own = [
                jnp.concatenate([prims[f, x + 4, :, cols], halo[f]], axis=0) for f in range(6)
            ]
            total = [jnp.zeros((ny, LANES), jnp.float32) for _ in range(nf)]
            for l in range(1, 5):
                ahead = [pltpu.roll(q, span - l, axis=0) for q in own]
                flux = pair_flux(own, ahead, 1, weights[l - 1])
                total = [
                    t + (v[:ny] - pltpu.roll(v, l, axis=0)[:ny]) for t, v in zip(total, flux)
                ]
            for f in range(nf):
                new = register_decay * reg[f, x, :, cols] + (acc[f, x, :, cols] + total[f])
                regout[ch, f, x] = new
                sec[ch, f, x] = state[f, x, :, cols] + register_gain * new

        @pl.loop(0, nf)
        def _(f):
            ahead = sec[ch, f, 0]
            back = sec[ch, f, nx - 1]
            for j in range(1, nx):
                ahead = sec[ch, f, j] + mu * ahead
                back = sec[ch, f, nx - 1 - j] + mu * back
            ab[ch, 0, f] = ahead
            ab[ch, 1, f] = back

    def section_copies(ch):
        return [
            remote(
                sec.at[ch, :, pl.ds(0, 2)],
                srecv.at[ch, 0],
                ss.at[ch, 0],
                sr.at[ch, 0],
                (prv, mine),
            ),
            remote(
                sec.at[ch, :, pl.ds(nx - 2, 2)],
                srecv.at[ch, 1],
                ss.at[ch, 1],
                sr.at[ch, 1],
                (nxt, mine),
            ),
        ]

    def ab_copy(ch):
        return remote(ab.at[ch], pab.at[ch], abs_.at[ch], abr.at[ch], (partner, mine))

    def chip_copies(ch):
        return [
            remote(
                chip.at[ch],
                chips.at[ch, d - 1],
                cs.at[ch, d - 1],
                cr.at[ch, d - 1],
                (chip_peer(d), mine),
            )
            for d in range(1, zs)
        ]

    def inc_copy(ch):
        return remote(inc.at[ch, core], pinc.at[ch], ins.at[ch], inr.at[ch], (partner, mine))

    scopies = [section_copies(ch) for ch in range(n_ch)]
    abcopies = [ab_copy(ch) for ch in range(n_ch)]
    ccopies = [chip_copies(ch) for ch in range(n_ch)]
    icopies = [inc_copy(ch) for ch in range(n_ch)]
    regcopies = [
        pltpu.make_async_copy(
            regout.at[ch],
            out_register.at[:, :, :, pl.ds(ch * LANES, LANES)],
            local.at[1 + ch],
        )
        for ch in range(n_ch)
    ]
    fcopies = [
        pltpu.make_async_copy(
            filt.at[ch],
            out_filtered.at[:, :, :, pl.ds(ch * LANES, LANES)],
            local.at[1 + n_ch + ch],
        )
        for ch in range(n_ch)
    ]

    def begin(ch):
        section_of(ch)
        abcopies[ch].start()
        for copy in scopies[ch]:
            copy.start()
        regcopies[ch].start()

    def across(ch):
        abcopies[ch].wait_recv()
        for f in range(nf):
            chip[ch, f] = pab[ch, core, f] + rho * ab[ch, core, f]
        for copy in ccopies[ch]:
            copy.start()

    def incoming(ch):
        for copy in ccopies[ch]:
            copy.wait_recv()
        scale = 1.0 / (1.0 - rho ** (2 * zs))
        for f in range(nf):
            total = (scale * rho ** (2 * (zs - 1))) * chip[ch, f]
            for d in range(1, zs):
                total = total + (scale * rho ** (2 * (d - 1))) * chips[ch, d - 1, f]
            inc[ch, core, f] = total
        icopies[ch].start()

    def finish(ch):
        icopies[ch].wait()
        for f in range(nf):
            inc[ch, 1 - core, f] = pab[ch, 1 - core, f] + rho * pinc[ch, f]
        for copy in scopies[ch]:
            copy.wait()

        @pl.loop(0, nf)
        def _(f):
            s = (
                [srecv[ch, 1, f, 0], srecv[ch, 1, f, 1]]
                + [sec[ch, f, j] for j in range(nx)]
                + [srecv[ch, 0, f, 0], srecv[ch, 0, f, 1]]
            )
            left = inc[ch, 0, f]
            for j in range(nx):
                left = s[j + 2] + mu * left
                near = (
                    stencil[0] * s[j + 2]
                    + stencil[1] * (s[j + 1] + s[j + 3])
                    + stencil[2] * (s[j] + s[j + 4])
                )
                filt[ch, f, j] = near + remainder * left
            right = inc[ch, 1, f]
            for j in reversed(range(nx)):
                filt[ch, f, j] = filt[ch, f, j] + (remainder * mu) * right
                right = s[j + 2] + mu * right

        fcopies[ch].start()

    for ch in range(n_ch):
        begin(ch)
        across(ch)
        if ch >= 1:
            incoming(ch - 1)
            finish(ch - 1)
    incoming(n_ch - 1)
    finish(n_ch - 1)

    for ch in range(n_ch):
        for copy in ycopies[ch]:
            copy.wait_send()
        abcopies[ch].wait_send()
        for copy in ccopies[ch]:
            copy.wait_send()
        regcopies[ch].wait()
        fcopies[ch].wait()
    for copy in xcopies:
        copy.wait_send()


def body(n_gx, n_yz, state, register):
    nf, nx, ny, nz = state.shape
    n_ch = nz // LANES
    zs = n_gx // 2
    f32 = jnp.float32
    dma = pltpu.SemaphoreType.DMA
    return pl.pallas_call(
        functools.partial(kernel, n_gx, n_yz),
        out_shape=[jax.ShapeDtypeStruct(state.shape, f32)] * 2,
        in_specs=[
            pl.BlockSpec(memory_space=pltpu.VMEM),
            pl.BlockSpec(memory_space=pl.ANY),
        ],
        out_specs=[pl.BlockSpec(memory_space=pl.ANY)] * 2,
        scratch_shapes=[
            pltpu.VMEM((nf, nx, ny, nz), f32),
            pltpu.VMEM((6, nx + 8, ny, nz), f32),
            pltpu.VMEM((nf, nx, ny, nz), f32),
            pltpu.VMEM((2, nf, 4, ny, nz), f32),
            pltpu.VMEM((n_ch, 2, nf, nx, 4, LANES), f32),
            pltpu.VMEM((n_ch, 2, nf, nx, 4, LANES), f32),
            pltpu.VMEM((n_ch, nf, nx, ny, LANES), f32),
            pltpu.VMEM((n_ch, nf, nx, ny, LANES), f32),
            pltpu.VMEM((n_ch, nf, nx, ny, LANES), f32),
            pltpu.VMEM((n_ch, 2, nf, 2, ny, LANES), f32),
            pltpu.VMEM((n_ch, 2, nf, ny, LANES), f32),
            pltpu.VMEM((n_ch, 2, nf, ny, LANES), f32),
            pltpu.VMEM((n_ch, nf, ny, LANES), f32),
            pltpu.VMEM((n_ch, zs - 1, nf, ny, LANES), f32),
            pltpu.VMEM((n_ch, 2, nf, ny, LANES), f32),
            pltpu.VMEM((n_ch, nf, ny, LANES), f32),
            dma((2,)),
            dma((2,)),
            dma((n_ch, 2)),
            dma((n_ch, 2)),
            dma((n_ch, 2)),
            dma((n_ch, 2)),
            dma((n_ch,)),
            dma((n_ch,)),
            dma((n_ch, zs - 1)),
            dma((n_ch, zs - 1)),
            dma((n_ch,)),
            dma((n_ch,)),
            dma((1 + 2 * n_ch,)),
        ],
        compiler_params=pltpu.CompilerParams(
            collective_id=0, has_side_effects=True, vmem_limit_bytes=40 * 1024 * 1024
        ),
    )(state, register)


def solution(mesh):
    spec = P(None, "gx", "yz", None)
    run = functools.partial(body, mesh.shape["gx"], mesh.shape["yz"])
    return jax.shard_map(
        lambda state, register: tuple(run(state, register)),
        mesh=mesh,
        in_specs=(spec, spec),
        out_specs=(spec, spec),
        check_vma=False,
    )
```

time: 124 us -> 37.3 us (0.30)
  between operations: 32.8 us -> 0.65 us
  Pallas kernels: 0 us -> 31.8 us
  waiting for transfers between devices: 30.4 us -> 0 us
  other arithmetic: 27 us -> 0 us
  local copies, waits for them, and re-layouts: 19.8 us -> 4.74 us
  starting transfers between devices: 10.6 us -> 0 us
  matrix products: 2.68 us -> 0 us
    pallas_call x0 -> x1, Pallas kernels: none -> 31.8 us  [body(): pl.pallas_call(functools.partial(kernel, n_gx, n_yz), out_shape=[jax.Shap...]
    all_gather x1 -> x0, waiting for transfers between devices: 15.9 us -> none  [share(): return lax.all_gather(pairs, 'gx', axis=0, tiled=True)]
    ppermute x6 -> x0, waiting for transfers between devices: 14.6 us -> none  [the longest x3 9.11 us: with_halo(): lax.ppermute(tail, axis, [(i, (i + 1) % count) for i in range(count)])]
    slice x83 -> x0, local copies, waits for them, and re-layouts: 11.5 us -> none  [the longest x52 3.9 us: residual_of(): ahead = tuple((jnp.roll(column, -offset, axis=2) for column in center))]
    ppermute x6 -> x0, starting transfers between devices: 10.5 us -> none  [the longest x3 10.5 us: with_halo(): lax.ppermute(head, axis, [((i + 1) % count, i) for i in range(count)])]
    div x4 -> x0, other arithmetic: 8.9 us -> none  [the longest x1 8.17 us: line_solve(): lax.linalg.tridiagonal_solve(lower, middle, upper, jnp.eye(inner, dtype=j...]
    add x4 -> x0, other arithmetic: 5.31 us -> none  [the longest x1 2.61 us: filter_rhs(): rhs + coeffs[shift] / 2.0 * (extended[:, 3 + shift:3 + shift + width_x] +...]
    mul x20 -> x0, other arithmetic: 4.8 us -> none  [the longest x10 2.69 us: pair_flux(): moment = [mass * speed_x, mass * speed_y, mass * speed_z]]
  transfers between devices with their start and end apart: 7 -> 0, of which waited for: 3 -> 0; matrix products, arithmetic and copies ran while one was open for 18% -> 0% of each run, Pallas kernels for 0% -> 0%
where the time goes in v1:
time: 37.3 us; the launch traced here: 37.2 us
  Pallas kernels  31.8 us (85%)
  local copies, waits for them, and re-layouts  4.74 us (13%)
  between operations  0.65 us (2%)
    pallas_call x1, Pallas kernels, body(): pl.pallas_call(functools.partial(kernel, n_gx, n_yz), out_shape=[jax.Shap...  31.8 us
    unnamed x6, local copies, waits for them, and re-layouts  4.74 us

profile of v1, /device:TPU:0, one launch (start us, length us, event | category | flops | bytes accessed | tf_op | source)
XLA Modules:
  0.0 37.2 jit_solution(8503895902645694208)
XLA Ops:
  0.6 0.0 copy-start
  0.6 1.3 %copy-done = f32[5,16,16,256]{3,2,1,0:T(8,128)S(1)} copy-done((f32[5,16,16,256]{3,2,1,0:T(8,128)S(1)}, f32[5,16,16,256]{3,2,1,0:T(8,128)}, u32[]{:S(2)}) %copy-start) | copy-done | bytes 1310744
  1.9 0.0 copy-start.1
  1.9 1.3 %copy-done.1 = f32[5,16,16,256]{3,2,1,0:T(8,128)S(1)} copy-done((f32[5,16,16,256]{3,2,1,0:T(8,128)S(1)}, f32[5,16,16,256]{3,2,1,0:T(8,128)}, u32[]{:S(2)}) %copy-start.1) | copy-done | bytes 1310744
  3.3 31.8 %shard_map.41 = (f32[5,16,16,256]{3,2,1,0:T(8,128)S(1)}, f32[5,16,16,256]{3,2,1,0:T(8,128)S(1)}) custom-call(f32[5,16,16,256]{3,2,1,0:T(8,128)S(1)} %copy-done, f32[5,16,16,256]{3,2,1,0:T(8,128)S(1)} %copy-done.1), custom_call_target="tpu_custom_call" | custom-call | tf_op jit(solution)/shard_map/pallas_call | solution.py:394
  35.0 1.1 %copy.6 = f32[5,16,16,256]{3,2,1,0:T(8,128)} copy(f32[5,16,16,256]{3,2,1,0:T(8,128)S(1)} %get-tuple-element.4) | data formatting | bytes 2621440
  36.1 1.1 %copy.7 = f32[5,16,16,256]{3,2,1,0:T(8,128)} copy(f32[5,16,16,256]{3,2,1,0:T(8,128)S(1)} %get-tuple-element.5) | data formatting | bytes 2621440
Async XLA Ops:
  0.6 1.3 %copy-start = (f32[5,16,16,256]{3,2,1,0:T(8,128)S(1)}, f32[5,16,16,256]{3,2,1,0:T(8,128)}, u32[]{:S(2)}) copy-start(f32[5,16,16,256]{3,2,1,0:T(8,128)} %state.1) | copy-start | bytes 3932164
  1.9 1.3 %copy-start.1 = (f32[5,16,16,256]{3,2,1,0:T(8,128)S(1)}, f32[5,16,16,256]{3,2,1,0:T(8,128)}, u32[]{:S(2)}) copy-start(f32[5,16,16,256]{3,2,1,0:T(8,128)} %register.1) | copy-start | bytes 3932164

commit v2 on v1

v2 whole, which is shorter than its diff:
```python
import functools

import jax
import jax.numpy as jnp
from jax import lax
from jax.experimental import pallas as pl
from jax.experimental.pallas import tpu as pltpu
from jax.sharding import PartitionSpec as P

gamma_gas = 1.4
central_weights = (4.0 / 5.0, -1.0 / 5.0, 4.0 / 105.0, -1.0 / 280.0)
filter_alpha = 0.49
register_decay = -5.0 / 9.0
register_gain = 15.0 / 16.0
time_step = 0.2
MESH = pl.DeviceIdType.MESH
LANES = 128
ROWS = 8


def filter_constants():
    alpha = filter_alpha
    a0 = (11.0 + 10.0 * alpha) / 16.0
    a1 = (15.0 + 34.0 * alpha) / 32.0
    a2 = (-3.0 + 6.0 * alpha) / 16.0
    a3 = (1.0 - 2.0 * alpha) / 32.0
    q2 = 4.0 * a3 / (2.0 * alpha)
    q1 = (2.0 * a2 - q2) / (2.0 * alpha)
    q0 = (a1 - 3.0 * a3 - q1) / (2.0 * alpha)
    rest = a0 - a2 - q0
    mu = (-1.0 + (1.0 - 4.0 * alpha * alpha) ** 0.5) / (2.0 * alpha)
    kappa = (1.0 + mu * mu) / (1.0 - mu * mu)
    return (q0 + 0.5 * q2, 0.5 * q1, 0.25 * q2), kappa * rest, mu


def primitives(fields):
    density = fields[0]
    inverse = 1.0 / density
    speeds = [fields[i] * inverse for i in (1, 2, 3)]
    kinetic = 0.5 * (
        fields[1] * speeds[0] + fields[2] * speeds[1] + fields[3] * speeds[2]
    )
    pressure = (gamma_gas - 1.0) * (fields[4] - kinetic)
    enthalpy = (fields[4] + pressure) * (0.5 * inverse)
    return [density] + [0.5 * speed for speed in speeds] + [pressure, enthalpy]


def pair_flux(left, right, direction, weight):
    density, speed_x, speed_y, speed_z, pressure, enthalpy = [
        one + other for one, other in zip(left, right)
    ]
    normal = (speed_x, speed_y, speed_z)[direction]
    mass = (weight * density) * normal
    moment = [mass * speed_x, mass * speed_y, mass * speed_z]
    moment[direction] = moment[direction] + weight * pressure
    return [mass] + moment + [mass * enthalpy]


def kernel(
    n_gx,
    n_yz,
    state_in,
    register_in,
    out_register,
    out_filtered,
    state,
    register,
    prims,
    acc,
    xrecv,
    ysend,
    yrecv,
    sec,
    early,
    filt,
    srecv,
    ab,
    pab,
    chip,
    chips,
    inc,
    pinc,
    xs,
    xr,
    ys,
    yr,
    ss,
    sr,
    abs_,
    abr,
    cs,
    cr,
    ins,
    inr,
    local,
):
    nf, nx, ny, nz = state.shape
    n_ch = nz // LANES
    tiles = ny // ROWS
    zs = n_gx // 2
    me = lax.axis_index("gx")
    mine = lax.axis_index("yz")
    core = lax.rem(me, 2)
    chip_at = lax.div(me, 2)
    nxt = lax.rem(me + 1, n_gx)
    prv = lax.rem(me + n_gx - 1, n_gx)
    partner = me + 1 - 2 * core
    ynxt = lax.rem(mine + 1, n_yz)
    yprv = lax.rem(mine + n_yz - 1, n_yz)

    def chip_peer(d):
        return 2 * lax.rem(chip_at + (1 - 2 * core) * d + zs, zs) + core

    barrier = pltpu.get_barrier_semaphore()
    peers = [(prv, mine), (nxt, mine), (me, yprv), (me, ynxt)]
    peers += [(chip_peer(d), mine) for d in range(1, zs)]
    for peer in peers:
        pl.semaphore_signal(barrier, inc=1, device_id=peer, device_id_type=MESH)

    loads = [
        pltpu.make_async_copy(state_in.at[f], state.at[f], local.at[f]) for f in range(nf)
    ]
    loads += [
        pltpu.make_async_copy(register_in.at[f], register.at[f], local.at[nf + f])
        for f in range(nf)
    ]
    for load in loads:
        load.start()

    for f in range(nf):
        loads[f].wait()

        @pl.loop(0, nx, unroll=4)
        def _(x, f=f):
            for ch in range(n_ch):
                cols = pl.ds(ch * LANES, LANES)
                ysend[ch, 0, f, x] = state[f, x, pl.ds(0, ROWS), cols][:4]
                ysend[ch, 1, f, x] = state[f, x, pl.ds(ny - ROWS, ROWS), cols][4:]

    pl.semaphore_wait(barrier, len(peers))

    def remote(src, dst, send, recv, peer):
        return pltpu.make_async_remote_copy(
            src_ref=src,
            dst_ref=dst,
            send_sem=send,
            recv_sem=recv,
            device_id=peer,
            device_id_type=MESH,
        )

    def y_copies(ch):
        return [
            remote(
                ysend.at[ch, side],
                yrecv.at[ch, side],
                ys.at[ch, side],
                yr.at[ch, side],
                (me, (yprv, ynxt)[side]),
            )
            for side in range(2)
        ]

    ycopies = [y_copies(ch) for ch in range(n_ch)]
    xcopies = [
        remote(state.at[:, pl.ds(0, 4)], xrecv.at[0], xs.at[0], xr.at[0], (prv, mine)),
        remote(state.at[:, pl.ds(nx - 4, 4)], xrecv.at[1], xs.at[1], xr.at[1], (nxt, mine)),
    ]
    for copy in ycopies[0] + xcopies:
        copy.start()
    for ch in range(1, n_ch):
        for copy in ycopies[ch]:
            copy.start()

    weights = [-time_step * w for w in central_weights]

    @pl.loop(0, nx * tiles)
    def _(i):
        x = i // tiles
        rows = pl.ds(pl.multiple_of((i % tiles) * ROWS, ROWS), ROWS)
        own = primitives([state[f, x, rows, :] for f in range(nf)])
        for f in range(6):
            prims[f, x + 4, rows, :] = own[f]
        total = [jnp.zeros((ROWS, nz), jnp.float32) for _ in range(nf)]
        for l in range(1, 5):
            ahead = [pltpu.roll(q, nz - l, axis=1) for q in own]
            flux = pair_flux(own, ahead, 2, weights[l - 1])
            total = [t + (v - pltpu.roll(v, l, axis=1)) for t, v in zip(total, flux)]
        for f in range(nf):
            acc[f, x, rows, :] = total[f]

    place = lax.broadcasted_iota(jnp.int32, (ny, LANES), 0)

    @pl.loop(0, nx)
    def _(x):
        for ch in range(n_ch):
            cols = pl.ds(ch * LANES, LANES)
            own = [prims[f, x + 4, :, cols] for f in range(6)]
            total = [acc[f, x, :, cols] for f in range(nf)]
            for l in range(1, 5):
                ahead = [pltpu.roll(q, ny - l, axis=0) for q in own]
                inside = jnp.where(place < ny - l, weights[l - 1], 0.0)
                flux = pair_flux(own, ahead, 1, inside)
                total = [t + (v - pltpu.roll(v, l, axis=0)) for t, v in zip(total, flux)]
            for f in range(nf):
                acc[f, x, :, cols] = total[f]

    for copy in xcopies:
        copy.wait_recv()

    @pl.loop(0, 4 * tiles)
    def _(i):
        x = i // tiles
        rows = pl.ds(pl.multiple_of((i % tiles) * ROWS, ROWS), ROWS)
        for side in range(2):
            got = primitives([xrecv[side, f, x, rows, :] for f in range(nf)])
            for f in range(6):
                prims[f, x + (nx + 4, 0)[side], rows, :] = got[f]

    for load in loads[nf:]:
        load.wait()

    stencil, remainder, mu = filter_constants()
    rho = mu**nx
    low = lax.broadcasted_iota(jnp.int32, (ROWS, LANES), 0) < 4
    top, bottom = pl.ds(0, ROWS), pl.ds(ny - ROWS, ROWS)

    def inner(first, last):
        return jnp.where(low, last, first)

    def outer(first, last):
        return jnp.where(low, first, last)

    def x_pass(ch):
        cols = pl.ds(ch * LANES, LANES)

        @pl.loop(0, nx)
        def _(x):
            parts = []
            for rows in (top, bottom):
                own = [prims[f, x + 4, rows, cols] for f in range(6)]
                total = [acc[f, x, rows, cols] for f in range(nf)]
                for l in range(1, 5):
                    ahead = [prims[f, x + 4 + l, rows, cols] for f in range(6)]
                    behind = [prims[f, x + 4 - l, rows, cols] for f in range(6)]
                    up = pair_flux(own, ahead, 0, weights[l - 1])
                    down = pair_flux(behind, own, 0, weights[l - 1])
                    total = [t + (u - d) for t, u, d in zip(total, up, down)]
                parts.append(
                    [
                        register_decay * register[f, x, rows, cols] + total[f]
                        for f in range(nf)
                    ]
                )
            for f in range(nf):
                first, last = parts[0][f], parts[1][f]
                state_first, state_last = state[f, x, top, cols], state[f, x, bottom, cols]
                for piece, pick in ((ch, inner), (n_ch + ch, outer)):
                    value = pick(first, last)
                    early[piece, f, x] = value
                    sec[piece, f, x] = pick(state_first, state_last) + register_gain * value

    signs = []
    spot = lax.broadcasted_iota(jnp.int32, (ROWS, LANES), 0)
    for l in range(1, 5):
        w = weights[l - 1]
        signs.append(jnp.where(spot < l, -w, jnp.where(spot >= ROWS - l, w, 0.0)))

    def y_pass(ch):
        piece = n_ch + ch
        cols = pl.ds(ch * LANES, LANES)
        for copy in ycopies[ch]:
            copy.wait_recv()

        @pl.loop(0, nx, unroll=2)
        def _(x):
            halo = primitives(
                [
                    jnp.concatenate([yrecv[ch, 0, f, x], yrecv[ch, 1, f, x]], axis=0)
                    for f in range(nf)
                ]
            )
            own = [
                outer(prims[f, x + 4, top, cols], prims[f, x + 4, bottom, cols])
                for f in range(6)
            ]
            total = [jnp.zeros((ROWS, LANES), jnp.float32) for _ in range(nf)]
            for l in range(1, 5):
                across = [
                    jnp.where(low, pltpu.roll(q, l, axis=0), pltpu.roll(q, ROWS - l, axis=0))
                    if l < 4
                    else pltpu.roll(q, l, axis=0)
                    for q in halo
                ]
                flux = pair_flux(own, across, 1, signs[l - 1])
                total = [t + v for t, v in zip(total, flux)]
            for f in range(nf):
                new = early[piece, f, x] + total[f]
                sec[piece, f, x] = sec[piece, f, x] + register_gain * total[f]
                mid = early[ch, f, x]
                out_register[f, x, top, cols] = jnp.where(low, new, mid)
                out_register[f, x, bottom, cols] = jnp.where(low, mid, new)

    def section_copies(p):
        return [
            remote(
                sec.at[p, :, pl.ds(0, 2)],
                srecv.at[p, 0],
                ss.at[p, 0],
                sr.at[p, 0],
                (prv, mine),
            ),
            remote(
                sec.at[p, :, pl.ds(nx - 2, 2)],
                srecv.at[p, 1],
                ss.at[p, 1],
                sr.at[p, 1],
                (nxt, mine),
            ),
        ]

    def chip_copies(p):
        return [
            remote(
                chip.at[p],
                chips.at[p, d - 1],
                cs.at[p, d - 1],
                cr.at[p, d - 1],
                (chip_peer(d), mine),
            )
            for d in range(1, zs)
        ]

    pieces = range(2 * n_ch)
    scopies = [section_copies(p) for p in pieces]
    abcopies = [
        remote(ab.at[p], pab.at[p], abs_.at[p], abr.at[p], (partner, mine)) for p in pieces
    ]
    ccopies = [chip_copies(p) for p in pieces]
    icopies = [
        remote(inc.at[p, core], pinc.at[p], ins.at[p], inr.at[p], (partner, mine))
        for p in pieces
    ]

    def begin(p):
        for f in range(nf):
            ahead = sec[p, f, 0]
            back = sec[p, f, nx - 1]
            for j in range(1, nx):
                ahead = sec[p, f, j] + mu * ahead
                back = sec[p, f, nx - 1 - j] + mu * back
            ab[p, 0, f] = ahead
            ab[p, 1, f] = back
        abcopies[p].start()
        for copy in scopies[p]:
            copy.start()

    def across_chips(p):
        abcopies[p].wait_recv()
        for f in range(nf):
            chip[p, f] = pab[p, core, f] + rho * ab[p, core, f]
        for copy in ccopies[p]:
            copy.start()

    def incoming(p):
        for copy in ccopies[p]:
            copy.wait_recv()
        scale = 1.0 / (1.0 - rho ** (2 * zs))
        for f in range(nf):
            total = (scale * rho ** (2 * (zs - 1))) * chip[p, f]
            for d in range(1, zs):
                total = total + (scale * rho ** (2 * (d - 1))) * chips[p, d - 1, f]
            inc[p, core, f] = total
        icopies[p].start()

    def finish(p):
        for copy in scopies[p]:
            copy.wait()
        icopies[p].wait()
        for f in range(nf):
            inc[p, 1 - core, f] = pab[p, 1 - core, f] + rho * pinc[p, f]
        for f in range(nf):
            s = (
                [srecv[p, 1, f, 0], srecv[p, 1, f, 1]]
                + [sec[p, f, j] for j in range(nx)]
                + [srecv[p, 0, f, 0], srecv[p, 0, f, 1]]
            )
            left = inc[p, 0, f]
            for j in range(nx):
                left = s[j + 2] + mu * left
                near = (
                    stencil[0] * s[j + 2]
                    + stencil[1] * (s[j + 1] + s[j + 3])
                    + stencil[2] * (s[j] + s[j + 4])
                )
                filt[p, f, j] = near + remainder * left
            right = inc[p, 1, f]
            for j in reversed(range(nx)):
                value = filt[p, f, j] + (remainder * mu) * right
                if p < n_ch:
                    filt[p, f, j] = value
                else:
                    mid = filt[p - n_ch, f, j]
                    cols = pl.ds((p - n_ch) * LANES, LANES)
                    out_filtered[f, j, top, cols] = jnp.where(low, value, mid)
                    out_filtered[f, j, bottom, cols] = jnp.where(low, mid, value)
                right = s[j + 2] + mu * right

    chunks = range(n_ch)
    for ch in chunks:
        x_pass(ch)
        begin(ch)
    for ch in chunks:
        across_chips(ch)
    y_pass(0)
    begin(n_ch)
    for ch in chunks:
        incoming(ch)
    across_chips(n_ch)
    for ch in chunks:
        finish(ch)
    for ch in range(1, n_ch):
        y_pass(ch)
        begin(n_ch + ch)
        incoming(n_ch + ch - 1)
        across_chips(n_ch + ch)
        finish(n_ch + ch - 1)
    incoming(2 * n_ch - 1)
    finish(2 * n_ch - 1)

    for ch in chunks:
        for copy in ycopies[ch]:
            copy.wait_send()
    for p in pieces:
        abcopies[p].wait_send()
        for copy in ccopies[p]:
            copy.wait_send()
    for copy in xcopies:
        copy.wait_send()


def body(n_gx, n_yz, state, register):
    nf, nx, ny, nz = state.shape
    n_ch = nz // LANES
    n_p = 2 * n_ch
    zs = n_gx // 2
    f32 = jnp.float32
    dma = pltpu.SemaphoreType.DMA
    return pl.pallas_call(
        functools.partial(kernel, n_gx, n_yz),
        out_shape=[jax.ShapeDtypeStruct(state.shape, f32)] * 2,
        in_specs=[pl.BlockSpec(memory_space=pltpu.HBM)] * 2,
        out_specs=[pl.BlockSpec(memory_space=pltpu.VMEM)] * 2,
        scratch_shapes=[
            pltpu.VMEM((nf, nx, ny, nz), f32),
            pltpu.VMEM((nf, nx, ny, nz), f32),
            pltpu.VMEM((6, nx + 8, ny, nz), f32),
            pltpu.VMEM((nf, nx, ny, nz), f32),
            pltpu.VMEM((2, nf, 4, ny, nz), f32),
            pltpu.VMEM((n_ch, 2, nf, nx, 4, LANES), f32),
            pltpu.VMEM((n_ch, 2, nf, nx, 4, LANES), f32),
            pltpu.VMEM((n_p, nf, nx, ROWS, LANES), f32),
            pltpu.VMEM((n_p, nf, nx, ROWS, LANES), f32),
            pltpu.VMEM((n_p, nf, nx, ROWS, LANES), f32),
            pltpu.VMEM((n_p, 2, nf, 2, ROWS, LANES), f32),
            pltpu.VMEM((n_p, 2, nf, ROWS, LANES), f32),
            pltpu.VMEM((n_p, 2, nf, ROWS, LANES), f32),
            pltpu.VMEM((n_p, nf, ROWS, LANES), f32),
            pltpu.VMEM((n_p, zs - 1, nf, ROWS, LANES), f32),
            pltpu.VMEM((n_p, 2, nf, ROWS, LANES), f32),
            pltpu.VMEM((n_p, nf, ROWS, LANES), f32),
            dma((2,)),
            dma((2,)),
            dma((n_ch, 2)),
            dma((n_ch, 2)),
            dma((n_p, 2)),
            dma((n_p, 2)),
            dma((n_p,)),
            dma((n_p,)),
            dma((n_p, zs - 1)),
            dma((n_p, zs - 1)),
            dma((n_p,)),
            dma((n_p,)),
            dma((2 * nf,)),
        ],
        compiler_params=pltpu.CompilerParams(
            collective_id=0, has_side_effects=True, vmem_limit_bytes=40 * 1024 * 1024
        ),
    )(state, register)


def solution(mesh):
    spec = P(None, "gx", "yz", None)
    run = functools.partial(body, mesh.shape["gx"], mesh.shape["yz"])
    return jax.shard_map(
        lambda state, register: tuple(run(state, register)),
        mesh=mesh,
        in_specs=(spec, spec),
        out_specs=(spec, spec),
        check_vma=False,
    )
```

time: 37.3 us -> 38.5 us (1.032)
  Pallas kernels: 31.8 us -> 33 us
    pallas_call x1, Pallas kernels: 31.8 us -> 33 us  [body(): pl.pallas_call(functools.partial(kernel, n_gx, n_yz), out_shape=[jax.Shap...]
where the time goes in v2:
time: 38.5 us; the launch traced here: 38.4 us
  Pallas kernels  33 us (86%)
  local copies, waits for them, and re-layouts  4.74 us (12%)
  between operations  0.65 us (2%)
    pallas_call x1, Pallas kernels, body(): pl.pallas_call(functools.partial(kernel, n_gx, n_yz), out_shape=[jax.Shap...  33 us
    unnamed x6, local copies, waits for them, and re-layouts  4.74 us

profile of v2, /device:TPU:0, one launch (start us, length us, event | category | flops | bytes accessed | tf_op | source)
XLA Modules:
  0.0 38.4 jit_solution(17418427061980185233)
XLA Ops:
  0.6 0.0 copy-start
  0.6 1.3 %copy-done = f32[5,16,16,256]{3,2,1,0:T(8,128)S(1)} copy-done((f32[5,16,16,256]{3,2,1,0:T(8,128)S(1)}, f32[5,16,16,256]{3,2,1,0:T(8,128)}, u32[]{:S(2)}) %copy-start) | copy-done | bytes 1310744
  1.9 0.0 copy-start.1
  1.9 1.3 %copy-done.1 = f32[5,16,16,256]{3,2,1,0:T(8,128)S(1)} copy-done((f32[5,16,16,256]{3,2,1,0:T(8,128)S(1)}, f32[5,16,16,256]{3,2,1,0:T(8,128)}, u32[]{:S(2)}) %copy-start.1) | copy-done | bytes 1310744
  3.3 33.0 %shard_map.41 = (f32[5,16,16,256]{3,2,1,0:T(8,128)S(1)}, f32[5,16,16,256]{3,2,1,0:T(8,128)S(1)}) custom-call(f32[5,16,16,256]{3,2,1,0:T(8,128)S(1)} %copy-done, f32[5,16,16,256]{3,2,1,0:T(8,128)S(1)} %copy-done.1), custom_call_target="tpu_custom_call" | custom-call | tf_op jit(solution)/shard_map/pallas_call | solution.py:449
  36.2 1.1 %copy.6 = f32[5,16,16,256]{3,2,1,0:T(8,128)} copy(f32[5,16,16,256]{3,2,1,0:T(8,128)S(1)} %get-tuple-element.4) | data formatting | bytes 2621440
  37.3 1.1 %copy.7 = f32[5,16,16,256]{3,2,1,0:T(8,128)} copy(f32[5,16,16,256]{3,2,1,0:T(8,128)S(1)} %get-tuple-element.5) | data formatting | bytes 2621440
Async XLA Ops:
  0.6 1.3 %copy-start = (f32[5,16,16,256]{3,2,1,0:T(8,128)S(1)}, f32[5,16,16,256]{3,2,1,0:T(8,128)}, u32[]{:S(2)}) copy-start(f32[5,16,16,256]{3,2,1,0:T(8,128)} %state_in.1) | copy-start | bytes 3932164
  1.9 1.3 %copy-start.1 = (f32[5,16,16,256]{3,2,1,0:T(8,128)S(1)}, f32[5,16,16,256]{3,2,1,0:T(8,128)}, u32[]{:S(2)}) copy-start(f32[5,16,16,256]{3,2,1,0:T(8,128)} %register_in.1) | copy-start | bytes 3932164

commit v3 on v2

--- a/solution.py
+++ b/solution.py
@@ -16,6 +16,8 @@
 MESH = pl.DeviceIdType.MESH
 LANES = 128
 ROWS = 8
+n_products = 18
+vmem_limit = 56 * 1024 * 1024
 
 
 def filter_constants():
@@ -31,6 +33,42 @@
     mu = (-1.0 + (1.0 - 4.0 * alpha * alpha) ** 0.5) / (2.0 * alpha)
     kappa = (1.0 + mu * mu) / (1.0 - mu * mu)
     return (q0 + 0.5 * q2, 0.5 * q1, 0.25 * q2), kappa * rest, mu
+
+
+def split_products(fields):
+    density, mom_x, mom_y, mom_z, energy = fields
+    inverse = 1.0 / density
+    u, v, w = mom_x * inverse, mom_y * inverse, mom_z * inverse
+    pressure = (gamma_gas - 1.0) * (energy - 0.5 * (mom_x * u + mom_y * v + mom_z * w))
+    total = energy + pressure
+    h = total * inverse
+    prims = [density, 0.5 * u, 0.5 * v, 0.5 * w, pressure, 0.5 * h]
+    return prims, [
+        density, w, mom_z,
+        mom_z * u, w * u, mom_x, u,
+        mom_z * v, w * v, mom_y, v,
+        mom_z * w, w * w,
+        mom_z * h, w * h, total, h,
+        pressure,
+    ]
+
+
+def split_residual(prims, d, scale):
+    density, u, v, w, _, h = prims
+    u, v, w, h = u + u, v + v, w + w, h + h
+    mom = density * w
+    mass = d[2] + density * d[1] + w * d[0]
+
+    def moment(q, d_mq, d_wq, d_rq, d_q):
+        return scale * (d_mq + density * d_wq + w * d_rq + q * mass + mom * d_q)
+
+    return [
+        (2.0 * scale) * mass,
+        moment(u, d[3], d[4], d[5], d[6]),
+        moment(v, d[7], d[8], d[9], d[10]),
+        moment(w, d[11], d[12], d[2], d[1]) + (4.0 * scale) * d[17],
+        moment(h, d[13], d[14], d[15], d[16]),
+    ]
 
 
 def primitives(fields):
@@ -93,6 +131,12 @@
     ins,
     inr,
     local,
+    matrix,
+    high,
+    rest,
+    deriv,
+    reg_out,
+    filt_out,
 ):
     nf, nx, ny, nz = state.shape
     n_ch = nz // LANES
@@ -127,6 +171,16 @@
     for load in loads:
         load.start()
 
+    gap = lax.broadcasted_iota(jnp.int32, (nz, nz), 0) - lax.broadcasted_iota(
+        jnp.int32, (nz, nz), 1
+    )
+    gap = jnp.where(gap < 0, gap + nz, gap)
+    entries = jnp.zeros((nz, nz), jnp.float32)
+    for l in range(1, 5):
+        whole = float(round(840.0 * central_weights[l - 1]))
+        entries = jnp.where(gap == l, whole, jnp.where(gap == nz - l, -whole, entries))
+    matrix[...] = entries.astype(jnp.bfloat16)
+
     for f in range(nf):
         loads[f].wait()
 
@@ -174,18 +228,32 @@
 
     weights = [-time_step * w for w in central_weights]
 
+    @pl.loop(0, nx)
+    def _(x):
+        rows = pl.ds(pl.multiple_of(x * ny, ny), ny)
+        own, products = split_products([state[f, x] for f in range(nf)])
+        for f in range(6):
+            prims[f, x + 4] = own[f]
+        for k, value in enumerate(products):
+            part = value.astype(jnp.bfloat16)
+            high[k, rows, :] = part
+            rest[k, rows, :] = (value - part.astype(jnp.float32)).astype(jnp.bfloat16)
+
+    @pl.loop(0, n_products)
+    def _(k):
+        whole = jnp.dot(high[k], matrix[...], preferred_element_type=jnp.float32)
+        deriv[k] = whole + jnp.dot(rest[k], matrix[...], preferred_element_type=jnp.float32)
+
     @pl.loop(0, nx * tiles)
     def _(i):
         x = i // tiles
         rows = pl.ds(pl.multiple_of((i % tiles) * ROWS, ROWS), ROWS)
-        own = primitives([state[f, x, rows, :] for f in range(nf)])
-        for f in range(6):
-            prims[f, x + 4, rows, :] = own[f]
-        total = [jnp.zeros((ROWS, nz), jnp.float32) for _ in range(nf)]
-        for l in range(1, 5):
-            ahead = [pltpu.roll(q, nz - l, axis=1) for q in own]
-            flux = pair_flux(own, ahead, 2, weights[l - 1])
-            total = [t + (v - pltpu.roll(v, l, axis=1)) for t, v in zip(total, flux)]
+        flat = pl.ds(pl.multiple_of(i * ROWS, ROWS), ROWS)
+        total = split_residual(
+            [prims[f, x + 4, rows, :] for f in range(6)],
+            [deriv[k, flat, :] for k in range(n_products)],
+            -time_step / (4.0 * 840.0),
+        )
         for f in range(nf):
             acc[f, x, rows, :] = total[f]
 
@@ -298,8 +366,8 @@
                 new = early[piece, f, x] + total[f]
                 sec[piece, f, x] = sec[piece, f, x] + register_gain * total[f]
                 mid = early[ch, f, x]
-                out_register[f, x, top, cols] = jnp.where(low, new, mid)
-                out_register[f, x, bottom, cols] = jnp.where(low, mid, new)
+                reg_out[f, x, top, cols] = jnp.where(low, new, mid)
+                reg_out[f, x, bottom, cols] = jnp.where(low, mid, new)
 
     def section_copies(p):
         return [
@@ -402,11 +470,23 @@
                 else:
                     mid = filt[p - n_ch, f, j]
                     cols = pl.ds((p - n_ch) * LANES, LANES)
-                    out_filtered[f, j, top, cols] = jnp.where(low, value, mid)
-                    out_filtered[f, j, bottom, cols] = jnp.where(low, mid, value)
+                    filt_out[f, j, top, cols] = jnp.where(low, value, mid)
+                    filt_out[f, j, bottom, cols] = jnp.where(low, mid, value)
                 right = s[j + 2] + mu * right
 
     chunks = range(n_ch)
+
+    def result_copy(src, dst, ch, sem):
+        cols = pl.ds(ch * LANES, LANES)
+        return pltpu.make_async_copy(
+            src.at[:, :, :, cols], dst.at[:, :, :, cols], local.at[sem]
+        )
+
+    reg_copies = [result_copy(reg_out, out_register, ch, 2 * nf + ch) for ch in chunks]
+    filt_copies = [
+        result_copy(filt_out, out_filtered, ch, 2 * nf + n_ch + ch) for ch in chunks
+    ]
+
     for ch in chunks:
         x_pass(ch)
         begin(ch)
@@ -414,6 +494,7 @@
         across_chips(ch)
     y_pass(0)
     begin(n_ch)
+    reg_copies[0].start()
     for ch in chunks:
         incoming(ch)
     across_chips(n_ch)
@@ -422,11 +503,14 @@
     for ch in range(1, n_ch):
         y_pass(ch)
         begin(n_ch + ch)
+        reg_copies[ch].start()
         incoming(n_ch + ch - 1)
         across_chips(n_ch + ch)
         finish(n_ch + ch - 1)
+        filt_copies[ch - 1].start()
     incoming(2 * n_ch - 1)
     finish(2 * n_ch - 1)
+    filt_copies[n_ch - 1].start()
 
     for ch in chunks:
         for copy in ycopies[ch]:
@@ -437,6 +521,19 @@
             copy.wait_send()
     for copy in xcopies:
         copy.wait_send()
+    for copy in reg_copies + filt_copies:
+        copy.wait()
+
+
+def hand_out(first, second, out_first, out_second, sems):
+    copies = []
+    for f in range(first.shape[0]):
+        for k, (src, dst) in enumerate(((first, out_first), (second, out_second))):
+            copies.append(pltpu.make_async_copy(src.at[f], dst.at[f], sems.at[k, f]))
+    for copy in copies:
+        copy.start()
+    for copy in copies:
+        copy.wait()
 
 
 def body(n_gx, n_yz, state, register):
@@ -446,11 +543,11 @@
     zs = n_gx // 2
     f32 = jnp.float32
     dma = pltpu.SemaphoreType.DMA
-    return pl.pallas_call(
+    results = pl.pallas_call(
         functools.partial(kernel, n_gx, n_yz),
         out_shape=[jax.ShapeDtypeStruct(state.shape, f32)] * 2,
-        in_specs=[pl.BlockSpec(memory_space=pltpu.HBM)] * 2,
-        out_specs=[pl.BlockSpec(memory_space=pltpu.VMEM)] * 2,
+        in_specs=[pl.BlockSpec(memory_space=pl.ANY)] * 2,
+        out_specs=[pl.BlockSpec(memory_space=pl.ANY)] * 2,
         scratch_shapes=[
             pltpu.VMEM((nf, nx, ny, nz), f32),
             pltpu.VMEM((nf, nx, ny, nz), f32),
@@ -481,12 +578,26 @@
             dma((n_p, zs - 1)),
             dma((n_p,)),
             dma((n_p,)),
-            dma((2 * nf,)),
+            dma((2 * nf + 2 * n_ch,)),
+            pltpu.VMEM((nz, nz), jnp.bfloat16),
+            pltpu.VMEM((n_products, nx * ny, nz), jnp.bfloat16),
+            pltpu.VMEM((n_products, nx * ny, nz), jnp.bfloat16),
+            pltpu.VMEM((n_products, nx * ny, nz), f32),
+            pltpu.VMEM((nf, nx, ny, nz), f32),
+            pltpu.VMEM((nf, nx, ny, nz), f32),
         ],
         compiler_params=pltpu.CompilerParams(
-            collective_id=0, has_side_effects=True, vmem_limit_bytes=40 * 1024 * 1024
+            collective_id=0, has_side_effects=True, vmem_limit_bytes=vmem_limit
         ),
     )(state, register)
+    return pl.pallas_call(
+        hand_out,
+        out_shape=[jax.ShapeDtypeStruct(state.shape, f32)] * 2,
+        in_specs=[pl.BlockSpec(memory_space=pl.ANY)] * 2,
+        out_specs=[pl.BlockSpec(memory_space=pl.ANY)] * 2,
+        scratch_shapes=[dma((2, nf))],
+        compiler_params=pltpu.CompilerParams(vmem_limit_bytes=vmem_limit),
+    )(*results)
 
 
 def solution(mesh):

time: 38.5 us -> 115 us (2.99)
  Pallas kernels: 33 us -> 114 us
  local copies, waits for them, and re-layouts: 4.74 us -> 0 us
    pallas_call x0 -> x1, Pallas kernels: none -> 80.6 us  [body(): pl.pallas_call(hand_out, out_shape=[jax.ShapeDtypeStruct(state.shape, f32...]
    unnamed x6 -> x0, local copies, waits for them, and re-layouts: 4.74 us -> none
where the time goes in v3:
time: 115 us
  Pallas kernels  114 us (99%)
    pallas_call x1, Pallas kernels, body(): pl.pallas_call(hand_out, out_shape=[jax.ShapeDtypeStruct(state.shape, f32...  80.6 us
    pallas_call x1, Pallas kernels, body(): pl.pallas_call(functools.partial(kernel, n_gx, n_yz), out_shape=[jax.Shap...  33.6 us

profile of v3, /device:TPU:0, one launch (start us, length us, event | category | flops | bytes accessed | tf_op | source)
XLA Modules:
  0.0 114.8 jit_solution(17189774206036723087)
XLA Ops:
  0.6 33.6 %shard_map.41 = (f32[5,16,16,256]{3,2,1,0:T(8,128)}, f32[5,16,16,256]{3,2,1,0:T(8,128)}) custom-call(f32[5,16,16,256]{3,2,1,0:T(8,128)} %state_in.1, f32[5,16,16,256]{3,2,1,0:T(8,128)} %register_in.1), custom_call_target="tpu_custom_call" | custom-call | tf_op jit(solution)/shard_map/pallas_call | solution.py:546
  34.2 80.6 %shard_map.42 = (f32[5,16,16,256]{3,2,1,0:T(8,128)}, f32[5,16,16,256]{3,2,1,0:T(8,128)}) custom-call(f32[5,16,16,256]{3,2,1,0:T(8,128)} %get-tuple-element.4.first, f32[5,16,16,256]{3,2,1,0:T(8,128)} %get-tuple-element.5.second), custom_call_target="tpu_custom_call" | custom-call | tf_op jit(solution)/shard_map/pallas_call | solution.py:593

commit v4 on v3

--- a/solution.py
+++ b/solution.py
@@ -17,7 +17,7 @@
 LANES = 128
 ROWS = 8
 n_products = 18
-vmem_limit = 56 * 1024 * 1024
+vmem_limit = 51 * 1024 * 1024
 
 
 def filter_constants():
@@ -99,8 +99,8 @@
     n_yz,
     state_in,
     register_in,
-    out_register,
-    out_filtered,
+    reg_out,
+    filt_out,
     state,
     register,
     prims,
@@ -135,8 +135,6 @@
     high,
     rest,
     deriv,
-    reg_out,
-    filt_out,
 ):
     nf, nx, ny, nz = state.shape
     n_ch = nz // LANES
@@ -476,41 +474,24 @@
 
     chunks = range(n_ch)
 
-    def result_copy(src, dst, ch, sem):
-        cols = pl.ds(ch * LANES, LANES)
-        return pltpu.make_async_copy(
-            src.at[:, :, :, cols], dst.at[:, :, :, cols], local.at[sem]
-        )
-
-    reg_copies = [result_copy(reg_out, out_register, ch, 2 * nf + ch) for ch in chunks]
-    filt_copies = [
-        result_copy(filt_out, out_filtered, ch, 2 * nf + n_ch + ch) for ch in chunks
-    ]
-
     for ch in chunks:
         x_pass(ch)
         begin(ch)
     for ch in chunks:
         across_chips(ch)
-    y_pass(0)
-    begin(n_ch)
-    reg_copies[0].start()
     for ch in chunks:
-        incoming(ch)
-    across_chips(n_ch)
-    for ch in chunks:
-        finish(ch)
-    for ch in range(1, n_ch):
         y_pass(ch)
         begin(n_ch + ch)
-        reg_copies[ch].start()
-        incoming(n_ch + ch - 1)
+        if ch == 0:
+            for early_piece in chunks:
+                incoming(early_piece)
+        else:
+            incoming(n_ch + ch - 1)
         across_chips(n_ch + ch)
-        finish(n_ch + ch - 1)
-        filt_copies[ch - 1].start()
+    for p in range(2 * n_ch - 1):
+        finish(p)
     incoming(2 * n_ch - 1)
     finish(2 * n_ch - 1)
-    filt_copies[n_ch - 1].start()
 
     for ch in chunks:
         for copy in ycopies[ch]:
@@ -521,19 +502,6 @@
             copy.wait_send()
     for copy in xcopies:
         copy.wait_send()
-    for copy in reg_copies + filt_copies:
-        copy.wait()
-
-
-def hand_out(first, second, out_first, out_second, sems):
-    copies = []
-    for f in range(first.shape[0]):
-        for k, (src, dst) in enumerate(((first, out_first), (second, out_second))):
-            copies.append(pltpu.make_async_copy(src.at[f], dst.at[f], sems.at[k, f]))
-    for copy in copies:
-        copy.start()
-    for copy in copies:
-        copy.wait()
 
 
 def body(n_gx, n_yz, state, register):
@@ -543,11 +511,11 @@
     zs = n_gx // 2
     f32 = jnp.float32
     dma = pltpu.SemaphoreType.DMA
-    results = pl.pallas_call(
+    return pl.pallas_call(
         functools.partial(kernel, n_gx, n_yz),
         out_shape=[jax.ShapeDtypeStruct(state.shape, f32)] * 2,
         in_specs=[pl.BlockSpec(memory_space=pl.ANY)] * 2,
-        out_specs=[pl.BlockSpec(memory_space=pl.ANY)] * 2,
+        out_specs=[pl.BlockSpec(memory_space=pltpu.VMEM)] * 2,
         scratch_shapes=[
             pltpu.VMEM((nf, nx, ny, nz), f32),
             pltpu.VMEM((nf, nx, ny, nz), f32),
@@ -578,26 +546,16 @@
             dma((n_p, zs - 1)),
             dma((n_p,)),
             dma((n_p,)),
-            dma((2 * nf + 2 * n_ch,)),
+            dma((2 * nf,)),
             pltpu.VMEM((nz, nz), jnp.bfloat16),
             pltpu.VMEM((n_products, nx * ny, nz), jnp.bfloat16),
             pltpu.VMEM((n_products, nx * ny, nz), jnp.bfloat16),
             pltpu.VMEM((n_products, nx * ny, nz), f32),
-            pltpu.VMEM((nf, nx, ny, nz), f32),
-            pltpu.VMEM((nf, nx, ny, nz), f32),
         ],
         compiler_params=pltpu.CompilerParams(
             collective_id=0, has_side_effects=True, vmem_limit_bytes=vmem_limit
         ),
     )(state, register)
-    return pl.pallas_call(
-        hand_out,
-        out_shape=[jax.ShapeDtypeStruct(state.shape, f32)] * 2,
-        in_specs=[pl.BlockSpec(memory_space=pl.ANY)] * 2,
-        out_specs=[pl.BlockSpec(memory_space=pl.ANY)] * 2,
-        scratch_shapes=[dma((2, nf))],
-        compiler_params=pltpu.CompilerParams(vmem_limit_bytes=vmem_limit),
-    )(*results)
 
 
 def solution(mesh):

time: 115 us -> 35.7 us (0.31)
  Pallas kernels: 114 us -> 32.8 us
  local copies, waits for them, and re-layouts: 0 us -> 2.11 us
    pallas_call x1 -> x0, Pallas kernels: 80.6 us -> none  [body(): pl.pallas_call(hand_out, out_shape=[jax.ShapeDtypeStruct(state.shape, f32...]
    unnamed x0 -> x2, local copies, waits for them, and re-layouts: none -> 2.11 us
where the time goes in v4:
time: 35.7 us; the launch traced here: 35.6 us
  Pallas kernels  32.8 us (92%)
  local copies, waits for them, and re-layouts  2.11 us (6%)
  between operations  0.64 us (2%)
    pallas_call x1, Pallas kernels, body(): pl.pallas_call(functools.partial(kernel, n_gx, n_yz), out_shape=[jax.Shap...  32.8 us
    unnamed x2, local copies, waits for them, and re-layouts  2.11 us

profile of v4, /device:TPU:0, one launch (start us, length us, event | category | flops | bytes accessed | tf_op | source)
XLA Modules:
  0.0 35.6 jit_solution(10595805287340590025)
XLA Ops:
  0.6 32.8 %shard_map.41 = (f32[5,16,16,256]{3,2,1,0:T(8,128)S(1)}, f32[5,16,16,256]{3,2,1,0:T(8,128)S(1)}) custom-call(f32[5,16,16,256]{3,2,1,0:T(8,128)} %state_in.1, f32[5,16,16,256]{3,2,1,0:T(8,128)} %register_in.1), custom_call_target="tpu_custom_call" | custom-call | tf_op jit(solution)/shard_map/pallas_call | solution.py:514
  33.5 1.1 %copy.6 = f32[5,16,16,256]{3,2,1,0:T(8,128)} copy(f32[5,16,16,256]{3,2,1,0:T(8,128)S(1)} %get-tuple-element.4) | data formatting | bytes 2621440
  34.5 1.1 %copy.7 = f32[5,16,16,256]{3,2,1,0:T(8,128)} copy(f32[5,16,16,256]{3,2,1,0:T(8,128)S(1)} %get-tuple-element.5) | data formatting | bytes 2621440

commit v5 on v4

--- a/solution.py
+++ b/solution.py
@@ -204,22 +204,31 @@
     def y_copies(ch):
         return [
             remote(
-                ysend.at[ch, side],
-                yrecv.at[ch, side],
-                ys.at[ch, side],
-                yr.at[ch, side],
+                ysend.at[ch, side, f],
+                yrecv.at[ch, side, f],
+                ys.at[ch, side, f],
+                yr.at[ch, side, f],
                 (me, (yprv, ynxt)[side]),
             )
+            for f in range(nf)
             for side in range(2)
         ]
 
     ycopies = [y_copies(ch) for ch in range(n_ch)]
     xcopies = [
-        remote(state.at[:, pl.ds(0, 4)], xrecv.at[0], xs.at[0], xr.at[0], (prv, mine)),
-        remote(state.at[:, pl.ds(nx - 4, 4)], xrecv.at[1], xs.at[1], xr.at[1], (nxt, mine)),
-    ]
-    for copy in ycopies[0] + xcopies:
-        copy.start()
+        remote(
+            state.at[f, pl.ds((0, nx - 4)[side], 4)],
+            xrecv.at[side, f],
+            xs.at[side, f],
+            xr.at[side, f],
+            ((prv, nxt)[side], mine),
+        )
+        for f in range(nf)
+        for side in range(2)
+    ]
+    for ycopy, xcopy in zip(ycopies[0], xcopies):
+        ycopy.start()
+        xcopy.start()
     for ch in range(1, n_ch):
         for copy in ycopies[ch]:
             copy.start()
@@ -534,10 +543,10 @@
             pltpu.VMEM((n_p, zs - 1, nf, ROWS, LANES), f32),
             pltpu.VMEM((n_p, 2, nf, ROWS, LANES), f32),
             pltpu.VMEM((n_p, nf, ROWS, LANES), f32),
-            dma((2,)),
-            dma((2,)),
-            dma((n_ch, 2)),
-            dma((n_ch, 2)),
+            dma((2, nf)),
+            dma((2, nf)),
+            dma((n_ch, 2, nf)),
+            dma((n_ch, 2, nf)),
             dma((n_p, 2)),
             dma((n_p, 2)),
             dma((n_p,)),

time: 35.7 us -> 36.1 us (1.011)
  Pallas kernels: 32.8 us -> 33.2 us
    pallas_call x1, Pallas kernels: 32.8 us -> 33.2 us  [body(): pl.pallas_call(functools.partial(kernel, n_gx, n_yz), out_shape=[jax.Shap...]
where the time goes in v5:
time: 36.1 us; the launch traced here: 36 us
  Pallas kernels  33.2 us (92%)
  local copies, waits for them, and re-layouts  2.11 us (6%)
  between operations  0.64 us (2%)
    pallas_call x1, Pallas kernels, body(): pl.pallas_call(functools.partial(kernel, n_gx, n_yz), out_shape=[jax.Shap...  33.2 us
    unnamed x2, local copies, waits for them, and re-layouts  2.11 us

profile of v5, /device:TPU:0, one launch (start us, length us, event | category | flops | bytes accessed | tf_op | source)
XLA Modules:
  0.0 36.0 jit_solution(5417967659663934628)
XLA Ops:
  0.6 33.2 %shard_map.41 = (f32[5,16,16,256]{3,2,1,0:T(8,128)S(1)}, f32[5,16,16,256]{3,2,1,0:T(8,128)S(1)}) custom-call(f32[5,16,16,256]{3,2,1,0:T(8,128)} %state_in.1, f32[5,16,16,256]{3,2,1,0:T(8,128)} %register_in.1), custom_call_target="tpu_custom_call" | custom-call | tf_op jit(solution)/shard_map/pallas_call | solution.py:523
  33.9 1.1 %copy.6 = f32[5,16,16,256]{3,2,1,0:T(8,128)} copy(f32[5,16,16,256]{3,2,1,0:T(8,128)S(1)} %get-tuple-element.4) | data formatting | bytes 2621440
  34.9 1.1 %copy.7 = f32[5,16,16,256]{3,2,1,0:T(8,128)} copy(f32[5,16,16,256]{3,2,1,0:T(8,128)S(1)} %get-tuple-element.5) | data formatting | bytes 2621440

commit v6 on v5

--- a/solution.py
+++ b/solution.py
@@ -92,6 +92,30 @@
     moment = [mass * speed_x, mass * speed_y, mass * speed_z]
     moment[direction] = moment[direction] + weight * pressure
     return [mass] + moment + [mass * enthalpy]
+
+
+def line_pass(low, high, first, last, direction, weights, get, put):
+    held, totals = {}, {}
+    for a in range(low, last):
+        for b in range(a, min(a + 5, high)):
+            if b not in held:
+                held[b] = get(b)
+        for l in range(1, 5):
+            b = a + l
+            if b >= high or (a < first and not first <= b < last):
+                continue
+            flux = pair_flux(held[a], held[b], direction, weights[l - 1])
+            if a >= first:
+                totals[a] = [t + v for t, v in zip(totals[a], flux)] if a in totals else flux
+            if first <= b < last:
+                totals[b] = (
+                    [t - v for t, v in zip(totals[b], flux)]
+                    if b in totals
+                    else [-v for v in flux]
+                )
+        if a >= first:
+            put(a, totals.pop(a))
+        held.pop(a)
 
 
 def kernel(
@@ -135,6 +159,8 @@
     high,
     rest,
     deriv,
+    yprims,
+    yacc,
 ):
     nf, nx, ny, nz = state.shape
     n_ch = nz // LANES
@@ -241,6 +267,8 @@
         own, products = split_products([state[f, x] for f in range(nf)])
         for f in range(6):
             prims[f, x + 4] = own[f]
+            for ch in range(n_ch):
+                yprims[f, ch, rows, :] = own[f][:, ch * LANES : (ch + 1) * LANES]
         for k, value in enumerate(products):
             part = value.astype(jnp.bfloat16)
             high[k, rows, :] = part
@@ -264,21 +292,26 @@
         for f in range(nf):
             acc[f, x, rows, :] = total[f]
 
-    place = lax.broadcasted_iota(jnp.int32, (ny, LANES), 0)
-
-    @pl.loop(0, nx)
-    def _(x):
-        for ch in range(n_ch):
-            cols = pl.ds(ch * LANES, LANES)
-            own = [prims[f, x + 4, :, cols] for f in range(6)]
-            total = [acc[f, x, :, cols] for f in range(nf)]
-            for l in range(1, 5):
-                ahead = [pltpu.roll(q, ny - l, axis=0) for q in own]
-                inside = jnp.where(place < ny - l, weights[l - 1], 0.0)
-                flux = pair_flux(own, ahead, 1, inside)
-                total = [t + (v - pltpu.roll(v, l, axis=0)) for t, v in zip(total, flux)]
-            for f in range(nf):
-                acc[f, x, :, cols] = total[f]
+    @pl.loop(0, n_ch * (nx // ROWS))
+    def _(i):
+        ch = i // (nx // ROWS)
+        base = (i % (nx // ROWS)) * (ROWS * ny)
+
+        def at(y):
+            return pl.ds(base + y, ROWS, stride=ny)
+
+        line_pass(
+            0,
+            ny,
+            0,
+            ny,
+            1,
+            weights,
+            lambda y: [yprims[f, ch, at(y), :] for f in range(6)],
+            lambda y, total: [
+                yacc.__setitem__((f, ch, at(y), slice(None)), total[f]) for f in range(nf)
+            ],
+        )
 
     for copy in xcopies:
         copy.wait_recv()
@@ -309,26 +342,36 @@
     def x_pass(ch):
         cols = pl.ds(ch * LANES, LANES)
 
-        @pl.loop(0, nx)
+        @pl.loop(0, tiles)
+        def _(i):
+            rows = pl.ds(pl.multiple_of(i * ROWS, ROWS), ROWS)
+
+            def put(x, total):
+                for f in range(nf):
+                    acc[f, x, rows, cols] = acc[f, x, rows, cols] + total[f]
+
+            line_pass(
+                -4,
+                nx + 4,
+                0,
+                nx,
+                0,
+                weights,
+                lambda x: [prims[f, x + 4, rows, cols] for f in range(6)],
+                put,
+            )
+
+        @pl.loop(0, nx, unroll=2)
         def _(x):
-            parts = []
-            for rows in (top, bottom):
-                own = [prims[f, x + 4, rows, cols] for f in range(6)]
-                total = [acc[f, x, rows, cols] for f in range(nf)]
-                for l in range(1, 5):
-                    ahead = [prims[f, x + 4 + l, rows, cols] for f in range(6)]
-                    behind = [prims[f, x + 4 - l, rows, cols] for f in range(6)]
-                    up = pair_flux(own, ahead, 0, weights[l - 1])
-                    down = pair_flux(behind, own, 0, weights[l - 1])
-                    total = [t + (u - d) for t, u, d in zip(total, up, down)]
-                parts.append(
-                    [
-                        register_decay * register[f, x, rows, cols] + total[f]
-                        for f in range(nf)
-                    ]
-                )
             for f in range(nf):
-                first, last = parts[0][f], parts[1][f]
+                ends = []
+                for k, rows in enumerate((top, bottom)):
+                    flat = pl.ds(pl.multiple_of(x * ny + k * (ny - ROWS), ROWS), ROWS)
+                    ends.append(
+                        register_decay * register[f, x, rows, cols]
+                        + (acc[f, x, rows, cols] + yacc[f, ch, flat, :])
+                    )
+                first, last = ends
                 state_first, state_last = state[f, x, top, cols], state[f, x, bottom, cols]
                 for piece, pick in ((ch, inner), (n_ch + ch, outer)):
                     value = pick(first, last)
@@ -560,6 +603,8 @@
             pltpu.VMEM((n_products, nx * ny, nz), jnp.bfloat16),
             pltpu.VMEM((n_products, nx * ny, nz), jnp.bfloat16),
             pltpu.VMEM((n_products, nx * ny, nz), f32),
+            pltpu.VMEM((6, n_ch, nx * ny, LANES), f32),
+            pltpu.VMEM((nf, n_ch, nx * ny, LANES), f32),
         ],
         compiler_params=pltpu.CompilerParams(
             collective_id=0, has_side_effects=True, vmem_limit_bytes=vmem_limit

time: 36.1 us -> 35.9 us (level)
  no operation moved by 1% of the time
where the time goes in v6:
time: 35.9 us; the launch traced here: 35.8 us
  Pallas kernels  33 us (92%)
  local copies, waits for them, and re-layouts  2.11 us (6%)
  between operations  0.64 us (2%)
    pallas_call x1, Pallas kernels, body(): pl.pallas_call(functools.partial(kernel, n_gx, n_yz), out_shape=[jax.Shap...  33 us
    unnamed x2, local copies, waits for them, and re-layouts  2.11 us

profile of v6, /device:TPU:0, one launch (start us, length us, event | category | flops | bytes accessed | tf_op | source)
XLA Modules:
  0.0 35.8 jit_solution(5518263460675684493)
XLA Ops:
  0.6 33.0 %shard_map.41 = (f32[5,16,16,256]{3,2,1,0:T(8,128)S(1)}, f32[5,16,16,256]{3,2,1,0:T(8,128)S(1)}) custom-call(f32[5,16,16,256]{3,2,1,0:T(8,128)} %state_in.1, f32[5,16,16,256]{3,2,1,0:T(8,128)} %register_in.1), custom_call_target="tpu_custom_call" | custom-call | tf_op jit(solution)/shard_map/pallas_call | solution.py:566
  33.7 1.1 %copy.6 = f32[5,16,16,256]{3,2,1,0:T(8,128)} copy(f32[5,16,16,256]{3,2,1,0:T(8,128)S(1)} %get-tuple-element.4) | data formatting | bytes 2621440
  34.7 1.1 %copy.7 = f32[5,16,16,256]{3,2,1,0:T(8,128)} copy(f32[5,16,16,256]{3,2,1,0:T(8,128)S(1)} %get-tuple-element.5) | data formatting | bytes 2621440

commit v7 on v6

--- a/solution.py
+++ b/solution.py
@@ -192,30 +192,8 @@
         pltpu.make_async_copy(register_in.at[f], register.at[f], local.at[nf + f])
         for f in range(nf)
     ]
-    for load in loads:
+    for load in loads[:nf]:
         load.start()
-
-    gap = lax.broadcasted_iota(jnp.int32, (nz, nz), 0) - lax.broadcasted_iota(
-        jnp.int32, (nz, nz), 1
-    )
-    gap = jnp.where(gap < 0, gap + nz, gap)
-    entries = jnp.zeros((nz, nz), jnp.float32)
-    for l in range(1, 5):
-        whole = float(round(840.0 * central_weights[l - 1]))
-        entries = jnp.where(gap == l, whole, jnp.where(gap == nz - l, -whole, entries))
-    matrix[...] = entries.astype(jnp.bfloat16)
-
-    for f in range(nf):
-        loads[f].wait()
-
-        @pl.loop(0, nx, unroll=4)
-        def _(x, f=f):
-            for ch in range(n_ch):
-                cols = pl.ds(ch * LANES, LANES)
-                ysend[ch, 0, f, x] = state[f, x, pl.ds(0, ROWS), cols][:4]
-                ysend[ch, 1, f, x] = state[f, x, pl.ds(ny - ROWS, ROWS), cols][4:]
-
-    pl.semaphore_wait(barrier, len(peers))
 
     def remote(src, dst, send, recv, peer):
         return pltpu.make_async_remote_copy(
@@ -252,12 +230,35 @@
         for f in range(nf)
         for side in range(2)
     ]
-    for ycopy, xcopy in zip(ycopies[0], xcopies):
-        ycopy.start()
-        xcopy.start()
+    pl.semaphore_wait(barrier, len(peers))
+    for f in range(nf):
+        loads[f].wait()
+
+        @pl.loop(0, nx, unroll=4)
+        def _(x, f=f):
+            for ch in range(n_ch):
+                cols = pl.ds(ch * LANES, LANES)
+                ysend[ch, 0, f, x] = state[f, x, pl.ds(0, ROWS), cols][:4]
+                ysend[ch, 1, f, x] = state[f, x, pl.ds(ny - ROWS, ROWS), cols][4:]
+
+        for k in (2 * f, 2 * f + 1):
+            ycopies[0][k].start()
+            xcopies[k].start()
     for ch in range(1, n_ch):
         for copy in ycopies[ch]:
             copy.start()
+    for load in loads[nf:]:
+        load.start()
+
+    gap = lax.broadcasted_iota(jnp.int32, (nz, nz), 0) - lax.broadcasted_iota(
+        jnp.int32, (nz, nz), 1
+    )
+    gap = jnp.where(gap < 0, gap + nz, gap)
+    entries = jnp.zeros((nz, nz), jnp.float32)
+    for l in range(1, 5):
+        whole = float(round(840.0 * central_weights[l - 1]))
+        entries = jnp.where(gap == l, whole, jnp.where(gap == nz - l, -whole, entries))
+    matrix[...] = entries.astype(jnp.bfloat16)
 
     weights = [-time_step * w for w in central_weights]
 
@@ -556,6 +557,17 @@
         copy.wait_send()
 
 
+def hand_out(first, second, out_first, out_second, sems):
+    copies = []
+    for k, (src, dst) in enumerate(((first, out_first), (second, out_second))):
+        for f in range(src.shape[0]):
+            copies.append(pltpu.make_async_copy(src.at[f], dst.at[f], sems.at[k, f]))
+    for copy in copies:
+        copy.start()
+    for copy in copies:
+        copy.wait()
+
+
 def body(n_gx, n_yz, state, register):
     nf, nx, ny, nz = state.shape
     n_ch = nz // LANES
@@ -563,7 +575,7 @@
     zs = n_gx // 2
     f32 = jnp.float32
     dma = pltpu.SemaphoreType.DMA
-    return pl.pallas_call(
+    results = pl.pallas_call(
         functools.partial(kernel, n_gx, n_yz),
         out_shape=[jax.ShapeDtypeStruct(state.shape, f32)] * 2,
         in_specs=[pl.BlockSpec(memory_space=pl.ANY)] * 2,
@@ -610,6 +622,13 @@
             collective_id=0, has_side_effects=True, vmem_limit_bytes=vmem_limit
         ),
     )(state, register)
+    return pl.pallas_call(
+        hand_out,
+        out_shape=[jax.ShapeDtypeStruct(state.shape, f32)] * 2,
+        in_specs=[pl.BlockSpec(memory_space=pltpu.VMEM)] * 2,
+        out_specs=[pl.BlockSpec(memory_space=pl.ANY)] * 2,
+        scratch_shapes=[dma((2, nf))],
+    )(*results)
 
 
 def solution(mesh):

time: 35.9 us -> 39.2 us (1.092)
  Pallas kernels: 33 us -> 36.3 us
    pallas_call x0 -> x1, Pallas kernels: none -> 3.27 us  [body(): pl.pallas_call(hand_out, out_shape=[jax.ShapeDtypeStruct(state.shape, f32...]
    unnamed x2 -> x4, local copies, waits for them, and re-layouts: 2.11 us -> 2.14 us
where the time goes in v7:
time: 39.2 us; the launch traced here: 39.1 us
  Pallas kernels  36.3 us (93%)
  local copies, waits for them, and re-layouts  2.14 us (5%)
  between operations  0.65 us (2%)
    pallas_call x1, Pallas kernels, body(): pl.pallas_call(functools.partial(kernel, n_gx, n_yz), out_shape=[jax.Shap...  33 us
    pallas_call x1, Pallas kernels, body(): pl.pallas_call(hand_out, out_shape=[jax.ShapeDtypeStruct(state.shape, f32...  3.27 us
    unnamed x4, local copies, waits for them, and re-layouts  2.14 us

profile of v7, /device:TPU:0, one launch (start us, length us, event | category | flops | bytes accessed | tf_op | source)
XLA Modules:
  0.0 39.1 jit_solution(9859132416222095737)
XLA Ops:
  0.6 33.0 %shard_map.41 = (f32[5,16,16,256]{3,2,1,0:T(8,128)S(1)}, f32[5,16,16,256]{3,2,1,0:T(8,128)S(1)}) custom-call(f32[5,16,16,256]{3,2,1,0:T(8,128)} %state_in.1, f32[5,16,16,256]{3,2,1,0:T(8,128)} %register_in.1), custom_call_target="tpu_custom_call" | custom-call | tf_op jit(solution)/shard_map/pallas_call | solution.py:578
  33.7 0.0 copy-start
  33.7 1.1 %copy-done = f32[5,16,16,256]{3,2,1,0:T(8,128)} copy-done((f32[5,16,16,256]{3,2,1,0:T(8,128)}, f32[5,16,16,256]{3,2,1,0:T(8,128)S(1)}, u32[]{:S(2)}) %copy-start) | copy-done | bytes 1310744
  34.7 0.0 copy-start.1
  34.7 1.1 %copy-done.1 = f32[5,16,16,256]{3,2,1,0:T(8,128)} copy-done((f32[5,16,16,256]{3,2,1,0:T(8,128)}, f32[5,16,16,256]{3,2,1,0:T(8,128)S(1)}, u32[]{:S(2)}) %copy-start.1) | copy-done | bytes 1310744
  35.8 3.3 %shard_map.42 = (f32[5,16,16,256]{3,2,1,0:T(8,128)}, f32[5,16,16,256]{3,2,1,0:T(8,128)}) custom-call(f32[5,16,16,256]{3,2,1,0:T(8,128)} %copy-done, f32[5,16,16,256]{3,2,1,0:T(8,128)} %copy-done.1), custom_call_target="tpu_custom_call" | custom-call | tf_op jit(solution)/shard_map/pallas_call | solution.py:625
Async XLA Ops:
  33.7 1.1 %copy-start = (f32[5,16,16,256]{3,2,1,0:T(8,128)}, f32[5,16,16,256]{3,2,1,0:T(8,128)S(1)}, u32[]{:S(2)}) copy-start(f32[5,16,16,256]{3,2,1,0:T(8,128)S(1)} %get-tuple-element.4.first) | copy-start | bytes 3932164
  34.7 1.1 %copy-start.1 = (f32[5,16,16,256]{3,2,1,0:T(8,128)}, f32[5,16,16,256]{3,2,1,0:T(8,128)S(1)}, u32[]{:S(2)}) copy-start(f32[5,16,16,256]{3,2,1,0:T(8,128)S(1)} %get-tuple-element.5.second) | copy-start | bytes 3932164

commit v8 on v7

--- a/solution.py
+++ b/solution.py
@@ -557,17 +557,6 @@
         copy.wait_send()
 
 
-def hand_out(first, second, out_first, out_second, sems):
-    copies = []
-    for k, (src, dst) in enumerate(((first, out_first), (second, out_second))):
-        for f in range(src.shape[0]):
-            copies.append(pltpu.make_async_copy(src.at[f], dst.at[f], sems.at[k, f]))
-    for copy in copies:
-        copy.start()
-    for copy in copies:
-        copy.wait()
-
-
 def body(n_gx, n_yz, state, register):
     nf, nx, ny, nz = state.shape
     n_ch = nz // LANES
@@ -575,7 +564,7 @@
     zs = n_gx // 2
     f32 = jnp.float32
     dma = pltpu.SemaphoreType.DMA
-    results = pl.pallas_call(
+    return pl.pallas_call(
         functools.partial(kernel, n_gx, n_yz),
         out_shape=[jax.ShapeDtypeStruct(state.shape, f32)] * 2,
         in_specs=[pl.BlockSpec(memory_space=pl.ANY)] * 2,
@@ -622,13 +611,6 @@
             collective_id=0, has_side_effects=True, vmem_limit_bytes=vmem_limit
         ),
     )(state, register)
-    return pl.pallas_call(
-        hand_out,
-        out_shape=[jax.ShapeDtypeStruct(state.shape, f32)] * 2,
-        in_specs=[pl.BlockSpec(memory_space=pltpu.VMEM)] * 2,
-        out_specs=[pl.BlockSpec(memory_space=pl.ANY)] * 2,
-        scratch_shapes=[dma((2, nf))],
-    )(*results)
 
 
 def solution(mesh):

time: 39.2 us -> 35.9 us (0.916)
  Pallas kernels: 36.3 us -> 33 us
    pallas_call x1 -> x0, Pallas kernels: 3.27 us -> none  [body(): pl.pallas_call(hand_out, out_shape=[jax.ShapeDtypeStruct(state.shape, f32...]
    unnamed x4 -> x2, local copies, waits for them, and re-layouts: 2.14 us -> 2.11 us
where the time goes in v8:
time: 35.9 us; the launch traced here: 35.8 us
  Pallas kernels  33 us (92%)
  local copies, waits for them, and re-layouts  2.11 us (6%)
  between operations  0.64 us (2%)
    pallas_call x1, Pallas kernels, body(): pl.pallas_call(functools.partial(kernel, n_gx, n_yz), out_shape=[jax.Shap...  33 us
    unnamed x2, local copies, waits for them, and re-layouts  2.11 us

profile of v8, /device:TPU:0, one launch (start us, length us, event | category | flops | bytes accessed | tf_op | source)
XLA Modules:
  0.0 35.8 jit_solution(14975620296111372677)
XLA Ops:
  0.6 33.0 %shard_map.41 = (f32[5,16,16,256]{3,2,1,0:T(8,128)S(1)}, f32[5,16,16,256]{3,2,1,0:T(8,128)S(1)}) custom-call(f32[5,16,16,256]{3,2,1,0:T(8,128)} %state_in.1, f32[5,16,16,256]{3,2,1,0:T(8,128)} %register_in.1), custom_call_target="tpu_custom_call" | custom-call | tf_op jit(solution)/shard_map/pallas_call | solution.py:567
  33.7 1.1 %copy.6 = f32[5,16,16,256]{3,2,1,0:T(8,128)} copy(f32[5,16,16,256]{3,2,1,0:T(8,128)S(1)} %get-tuple-element.4) | data formatting | bytes 2621440
  34.7 1.1 %copy.7 = f32[5,16,16,256]{3,2,1,0:T(8,128)} copy(f32[5,16,16,256]{3,2,1,0:T(8,128)S(1)} %get-tuple-element.5) | data formatting | bytes 2621440
